TPU v7x, 32 devices: a whole 2x2x4 slice. The times are simulated.
32 devices in a mesh: seq: 1, ctx: 16 (over z, y, x), wsh: 2 (over core).
Axes of the slice: x: 2, y: 2, z: 4, core: 2. Of those that a mesh axis runs over, the one named last changes fastest.
Arguments:
- tokens: bfloat16 [4096, 1472], P(('seq', 'ctx', 'wsh')), may hold values from -6 to 6
- encoded: bfloat16 [2048, 1472], P(('seq', 'ctx', 'wsh')), may hold values from -6 to 6
- cotangent: bfloat16 [4096, 1472], P(('seq', 'ctx', 'wsh')), may hold values from -6 to 6
- assign: int32 [16], replicated, may hold values from 0 to 15, each once
- bucket_ids: int32 [4096], replicated, may hold values from 0 to 31, never falling along the last dimension, each value on 1 to 512 neighbouring positions
- gain_self: bfloat16 [1472], P('wsh'), may hold values from 0.5 to 1.5
- gain_cross: bfloat16 [1472], P('wsh'), may hold values from 0.5 to 1.5
- gain_ffn: bfloat16 [1472], P('wsh'), may hold values from 0.5 to 1.5
- query_weight: bfloat16 [1472, 384], P('wsh'), may hold values from -0.078125 to 0.078125
- key_weight: bfloat16 [1472, 384], P('wsh'), may hold values from -0.078125 to 0.078125
- value_weight: bfloat16 [1472, 384], P('wsh'), may hold values from -0.15625 to 0.15625
- out_weight: bfloat16 [384, 1472], P('wsh'), may hold values from -1.5 to 1.5
- cross_query: bfloat16 [1472, 384], P('wsh'), may hold values from -0.078125 to 0.078125
- cross_key: bfloat16 [1472, 384], P('wsh'), may hold values from -0.078125 to 0.078125
- cross_value: bfloat16 [1472, 384], P('wsh'), may hold values from -0.15625 to 0.15625
- cross_out: bfloat16 [384, 1472], P('wsh'), may hold values from -2 to 2
- gate_weight: bfloat16 [1472, 3584], P('wsh'), may hold values from -0.15625 to 0.15625
- up_weight: bfloat16 [1472, 3584], P('wsh'), may hold values from -0.15625 to 0.15625
- down_weight: bfloat16 [3584, 1472], P('wsh'), may hold values from -0.09375 to 0.09375
- bucket_table: bfloat16 [32, 6], replicated, may hold values from -4 to 4
Outputs:
- output: bfloat16 [4096, 1472], P(('seq', 'ctx', 'wsh'))
- tokens_grad: float32 [4096, 1472], P(('seq', 'ctx', 'wsh'))
- encoded_grad: float32 [2048, 1472], P(('seq', 'ctx', 'wsh'))
- gain_self_grad: float32 [1472], P('seq')
- gain_cross_grad: float32 [1472], P('seq')
- gain_ffn_grad: float32 [1472], P('seq')
- query_weight_grad: float32 [1472, 384], P('seq', ('ctx', 'wsh'))
- key_weight_grad: float32 [1472, 384], P('seq', ('ctx', 'wsh'))
- value_weight_grad: float32 [1472, 384], P('seq', ('ctx', 'wsh'))
- out_weight_grad: float32 [384, 1472], P(('seq', 'ctx', 'wsh'))
- cross_query_grad: float32 [1472, 384], P('seq', ('ctx', 'wsh'))
- cross_key_grad: float32 [1472, 384], P('seq', ('ctx', 'wsh'))
- cross_value_grad: float32 [1472, 384], P('seq', ('ctx', 'wsh'))
- cross_out_grad: float32 [384, 1472], P(('seq', 'ctx', 'wsh'))
- gate_weight_grad: float32 [1472, 3584], P('seq', ('ctx', 'wsh'))
- up_weight_grad: float32 [1472, 3584], P('seq', ('ctx', 'wsh'))
- down_weight_grad: float32 [3584, 1472], P(('seq', 'ctx', 'wsh'))
- bucket_table_grad: float32 [32, 6], P('seq')
Inputs may be any that keep to these rules, and one draw needn't show every extreme that they name: `assign`: each early block 0 to 15 belongs to exactly one index of ctx, which also holds block 31 minus it. `bucket_ids`: starts at 0 and never falls as the distance grows; every bucket covers 1 to 512 consecutive distances, one exactly that many.
All inputs are finite; a program needn't handle non-finite values.
Results may differ from a plain program's by a relative error of at most 0.03.
The roundings to bfloat16 on the way count: a program that leaves them out, or rounds other values in their place, can miss the bound.
Values may be sent and summed in bfloat16 or wider, within the bound.
No kernel may reach another device: no remote copies, remote signals or barrier semaphores. Data moves between devices by JAX's collectives and lax.ppermute only.
A program may use at most 320 MiB of HBM per device.

v0:
```python
import jax
import jax.numpy as jnp
from jax import lax
from jax.sharding import PartitionSpec as P

EPS = 1e-06
NEG = -1e30


def root_norm(inputs, gain_vec):
    return inputs * lax.rsqrt(jnp.mean(inputs * inputs, axis=-1, keepdims=True) + EPS) * gain_vec


def product(first_op, second_op):
    return jnp.dot(first_op, second_op, preferred_element_type=jnp.float32)


def product_tn(first_op, second_op):
    return lax.dot_general(
        first_op, second_op, (((0,), (0,)), ((), ())), preferred_element_type=jnp.float32
    )


def product_nt(first_op, second_op):
    return lax.dot_general(
        first_op, second_op, (((1,), (1,)), ((), ())), preferred_element_type=jnp.float32
    )


def heads_first(matrix, head_count):
    return jnp.transpose(
        matrix.reshape(matrix.shape[0], head_count, matrix.shape[1] // head_count), (1, 0, 2)
    )


def heads_joined(tensor):
    return jnp.transpose(tensor, (1, 0, 2)).reshape(
        tensor.shape[1], tensor.shape[0] * tensor.shape[2]
    )


def local(
    tokens,
    encoded,
    cotangent,
    assign,
    bucket_ids,
    gain_self,
    gain_cross,
    gain_ffn,
    query_weight,
    key_weight,
    value_weight,
    out_weight,
    cross_query,
    cross_key,
    cross_value,
    cross_out,
    gate_weight,
    up_weight,
    down_weight,
    bucket_table,
):
    ctx_count = lax.axis_size("ctx")
    wsh_count = lax.axis_size("wsh")
    ctx_index = lax.axis_index("ctx")
    wsh_index = lax.axis_index("wsh")
    tok_rows = tokens.shape[0]
    half_rows = tok_rows // 2
    block_rows = half_rows * wsh_count
    seq_len = block_rows * 2 * ctx_count
    key_tile = min(2048, seq_len)
    tile_total = seq_len // key_tile
    head_count = bucket_table.shape[1]
    bucket_count = bucket_table.shape[0]
    (
        full_gain_self,
        full_gain_cross,
        full_gain_ffn,
        full_query,
        full_key,
        full_value,
        full_out,
        full_cross_query,
        full_cross_key,
        full_cross_value,
        full_cross_out,
        full_gate,
        full_up,
        full_down,
    ) = (
        lax.all_gather(gain_self, "wsh", axis=0, tiled=True),
        lax.all_gather(gain_cross, "wsh", axis=0, tiled=True),
        lax.all_gather(gain_ffn, "wsh", axis=0, tiled=True),
        lax.all_gather(query_weight, "wsh", axis=0, tiled=True),
        lax.all_gather(key_weight, "wsh", axis=0, tiled=True),
        lax.all_gather(value_weight, "wsh", axis=0, tiled=True),
        lax.all_gather(out_weight, "wsh", axis=0, tiled=True),
        lax.all_gather(cross_query, "wsh", axis=0, tiled=True),
        lax.all_gather(cross_key, "wsh", axis=0, tiled=True),
        lax.all_gather(cross_value, "wsh", axis=0, tiled=True),
        lax.all_gather(cross_out, "wsh", axis=0, tiled=True),
        lax.all_gather(gate_weight, "wsh", axis=0, tiled=True),
        lax.all_gather(up_weight, "wsh", axis=0, tiled=True),
        lax.all_gather(down_weight, "wsh", axis=0, tiled=True),
    )
    inner_width = full_query.shape[1]
    head_size = inner_width // head_count
    gain_one = full_gain_self.astype(jnp.float32)
    gain_two = full_gain_cross.astype(jnp.float32)
    gain_three = full_gain_ffn.astype(jnp.float32)
    early_block = jnp.take(assign, ctx_index)
    late_block = 2 * ctx_count - 1 - early_block
    inside = jnp.arange(half_rows, dtype=jnp.int32) + wsh_index * half_rows
    local_pos = jnp.concatenate(
        [early_block * block_rows + inside, late_block * block_rows + inside]
    )
    pos_rows = local_pos[None, :]
    natural = jnp.arange(seq_len, dtype=jnp.int32)
    block_of = natural // block_rows
    within = natural % block_rows
    lanes = jnp.arange(ctx_count, dtype=jnp.int32)
    owner_early = jnp.sum(jnp.where(assign[None, :] == lanes[:, None], lanes[None, :], 0), axis=1)
    is_late = (block_of >= ctx_count).astype(jnp.int32)
    paired = jnp.where(is_late == 1, 2 * ctx_count - 1 - block_of, block_of)
    owner = jnp.take(owner_early, paired)
    device_row = (
        (owner * wsh_count + within // half_rows) * 2 + is_late
    ) * half_rows + within % half_rows
    bucket_lanes = jnp.arange(bucket_count, dtype=jnp.int32)
    bucket_first = jnp.sum((bucket_ids[None, :] < bucket_lanes[:, None]).astype(jnp.int32), axis=1)
    bucket_after = jnp.concatenate([bucket_first[1:], jnp.full((1,), seq_len + 1, jnp.int32)])

    def bucket_hot(clipped):
        spread = clipped[:, :, None]
        return (
            (spread >= bucket_first[None, None, :]) & (spread < bucket_after[None, None, :])
        ).astype(jnp.bfloat16)

    def bucket_bias(hot):
        return jnp.einsum("qkb,bh->hqk", hot, bucket_table, preferred_element_type=jnp.float32)

    x_float = tokens.astype(jnp.float32)
    normed_one = root_norm(x_float, gain_one).astype(jnp.bfloat16)
    queries = product(normed_one, full_query).astype(jnp.bfloat16)
    keys_local = product(normed_one, full_key).astype(jnp.bfloat16)
    values_local = product(normed_one, full_value).astype(jnp.bfloat16)
    keys_all, values_all = (
        lax.all_gather(keys_local, ("ctx", "wsh"), axis=0, tiled=True),
        lax.all_gather(values_local, ("ctx", "wsh"), axis=0, tiled=True),
    )
    keys_nat = jnp.take(keys_all, device_row, axis=0).reshape(seq_len, head_count, head_size)
    values_nat = jnp.take(values_all, device_row, axis=0).reshape(seq_len, head_count, head_size)
    query_heads = heads_first(queries, head_count)
    early_tiles = ((early_block + 1) * block_rows + key_tile - 1) // key_tile
    all_tiles = ((late_block + 1) * block_rows + key_tile - 1) // key_tile

    def tile_scores(query_rows, pos_in, offset):
        key_block = lax.dynamic_slice_in_dim(keys_nat, offset, key_tile, 0)
        raw_scores = jnp.einsum(
            "hqd,khd->hqk", query_rows, key_block, preferred_element_type=jnp.float32
        )
        distance = pos_in[:, None] - (offset + jnp.arange(key_tile, dtype=jnp.int32))[None, :]
        hot = bucket_hot(jnp.maximum(distance, 0))
        return (jnp.where((distance >= 0)[None], raw_scores + bucket_bias(hot), NEG), hot)

    def late_rows(tree):
        return jax.tree.map(lambda member: member[:, half_rows:], tree)

    def sweep(advance, rows_in, row_state, shared):
        carried = lax.fori_loop(
            0,
            early_tiles,
            lambda tile_no, carried_in: advance(tile_no, rows_in, carried_in),
            (row_state, shared),
        )
        late_in = late_rows(rows_in)
        late_state, shared = lax.fori_loop(
            early_tiles,
            all_tiles,
            lambda tile_no, carried_in: advance(tile_no, late_in, carried_in),
            (late_rows(carried[0]), carried[1]),
        )
        merged = jax.tree.map(
            lambda entire, portion: jnp.concatenate([entire[:, :half_rows], portion], axis=1),
            carried[0],
            late_state,
        )
        return (merged, shared)

    def stats_step(tile_no, rows_in, carried):
        (run_max, run_sum), shared = carried
        query_rows, pos_in = rows_in
        scores, hot = tile_scores(query_rows, pos_in[0], tile_no * key_tile)
        new_max = jnp.maximum(run_max, jnp.max(scores, axis=2))
        run_sum = run_sum * jnp.exp(run_max - new_max) + jnp.sum(
            jnp.exp(scores - new_max[:, :, None]), axis=2
        )
        return ((new_max, run_sum), shared)

    zero_stats = jnp.zeros((head_count, tok_rows), jnp.float32)
    stats_out = sweep(stats_step, (query_heads, pos_rows), (zero_stats + NEG, zero_stats), ())
    self_lse = stats_out[0][0] + jnp.log(stats_out[0][1])

    def value_step(tile_no, rows_in, carried):
        (accumulated,), shared = carried
        query_rows, pos_in, lse_rows = rows_in
        offset = tile_no * key_tile
        scores, hot = tile_scores(query_rows, pos_in[0], offset)
        prob_tile = jnp.exp(scores - lse_rows[:, :, None]).astype(jnp.bfloat16)
        value_block = lax.dynamic_slice_in_dim(values_nat, offset, key_tile, 0)
        accumulated = accumulated + jnp.einsum(
            "hqk,khd->hqd", prob_tile, value_block, preferred_element_type=jnp.float32
        )
        return ((accumulated,), shared)

    zero_heads = jnp.zeros((head_count, tok_rows, head_size), jnp.float32)
    value_out = sweep(value_step, (query_heads, pos_rows, self_lse), (zero_heads,), ())
    attended = heads_joined(value_out[0][0]).astype(jnp.bfloat16)
    hidden_one = x_float + product(attended, full_out)
    normed_two = root_norm(hidden_one, gain_two).astype(jnp.bfloat16)
    cross_queries = product(normed_two, full_cross_query).astype(jnp.bfloat16)
    enc_keys_local = product(encoded, full_cross_key).astype(jnp.bfloat16)
    enc_values_local = product(encoded, full_cross_value).astype(jnp.bfloat16)
    enc_keys, enc_values = (
        lax.all_gather(enc_keys_local, ("ctx", "wsh"), axis=0, tiled=True),
        lax.all_gather(enc_values_local, ("ctx", "wsh"), axis=0, tiled=True),
    )
    enc_keys_h = enc_keys.reshape(enc_keys.shape[0], head_count, head_size)
    enc_values_h = enc_values.reshape(enc_values.shape[0], head_count, head_size)
    cross_heads = heads_first(cross_queries, head_count)
    cross_scores = jnp.einsum(
        "hqd,khd->hqk", cross_heads, enc_keys_h, preferred_element_type=jnp.float32
    )
    cross_max = jnp.max(cross_scores, axis=2, keepdims=True)
    cross_lse = cross_max + jnp.log(
        jnp.sum(jnp.exp(cross_scores - cross_max), axis=2, keepdims=True)
    )
    cross_probs = jnp.exp(cross_scores - cross_lse).astype(jnp.bfloat16)
    cross_attended = heads_joined(
        jnp.einsum("hqk,khd->hqd", cross_probs, enc_values_h, preferred_element_type=jnp.float32)
    ).astype(jnp.bfloat16)
    hidden_two = hidden_one + product(cross_attended, full_cross_out)
    normed_three = root_norm(hidden_two, gain_three).astype(jnp.bfloat16)
    gate = product(normed_three, full_gate)
    up_proj = product(normed_three, full_up)
    activated = (jax.nn.gelu(gate, approximate=True) * up_proj).astype(jnp.bfloat16)
    output = (hidden_two + product(activated, full_down)).astype(jnp.bfloat16)
    grad_out = cotangent.astype(jnp.float32)
    down_grad = product_tn(activated, cotangent)
    grad_activated = product_nt(cotangent, full_down)
    gelu_out, gelu_pull = jax.vjp(
        lambda gate_in, up_in: jax.nn.gelu(gate_in, approximate=True) * up_in, gate, up_proj
    )
    grad_gate, grad_up = gelu_pull(grad_activated)
    grad_gate = grad_gate.astype(jnp.bfloat16)
    grad_up = grad_up.astype(jnp.bfloat16)
    gate_grad = product_tn(normed_three, grad_gate)
    up_grad = product_tn(normed_three, grad_up)
    grad_normed_three = product_nt(grad_gate, full_gate) + product_nt(grad_up, full_up)
    norm_out, norm_pull = jax.vjp(root_norm, hidden_two, gain_three)
    grad_two_part, gain_three_grad = norm_pull(grad_normed_three)
    grad_two = grad_out + grad_two_part
    grad_y_two = grad_two.astype(jnp.bfloat16)
    cross_out_grad = product_tn(cross_attended, grad_y_two)
    grad_cross_att = heads_first(
        product_nt(grad_y_two, full_cross_out).astype(jnp.bfloat16), head_count
    )
    cross_back = jnp.exp(
        jnp.einsum("hqd,khd->hqk", cross_heads, enc_keys_h, preferred_element_type=jnp.float32)
        - cross_lse
    )
    cross_grad_probs = jnp.einsum(
        "hqd,khd->hqk", grad_cross_att, enc_values_h, preferred_element_type=jnp.float32
    )
    cross_delta = jnp.sum(cross_back * cross_grad_probs, axis=2, keepdims=True)
    cross_dscore = (cross_back * (cross_grad_probs - cross_delta)).astype(jnp.bfloat16)
    grad_cross_query = heads_joined(
        jnp.einsum("hqk,khd->hqd", cross_dscore, enc_keys_h, preferred_element_type=jnp.float32)
    ).astype(jnp.bfloat16)
    enc_key_term = jnp.einsum(
        "hqk,hqd->khd", cross_dscore, cross_heads, preferred_element_type=jnp.float32
    ).reshape(enc_keys.shape[0], inner_width)
    enc_value_term = jnp.einsum(
        "hqk,hqd->khd",
        cross_back.astype(jnp.bfloat16),
        grad_cross_att,
        preferred_element_type=jnp.float32,
    ).reshape(enc_keys.shape[0], inner_width)
    enc_key_sum, enc_value_sum = (
        lax.psum_scatter(enc_key_term, ("ctx", "wsh"), scatter_dimension=0, tiled=True),
        lax.psum_scatter(enc_value_term, ("ctx", "wsh"), scatter_dimension=0, tiled=True),
    )
    enc_key_grad = enc_key_sum.astype(jnp.bfloat16)
    enc_value_grad = enc_value_sum.astype(jnp.bfloat16)
    cross_key_grad = product_tn(encoded, enc_key_grad)
    cross_value_grad = product_tn(encoded, enc_value_grad)
    encoded_grad = product_nt(enc_key_grad, full_cross_key) + product_nt(
        enc_value_grad, full_cross_value
    )
    cross_query_grad = product_tn(normed_two, grad_cross_query)
    grad_normed_two = product_nt(grad_cross_query, full_cross_query)
    norm_out, norm_pull = jax.vjp(root_norm, hidden_one, gain_two)
    grad_one_part, gain_two_grad = norm_pull(grad_normed_two)
    grad_one = grad_two + grad_one_part
    grad_y_one = grad_one.astype(jnp.bfloat16)
    out_grad = product_tn(attended, grad_y_one)
    grad_att = product_nt(grad_y_one, full_out).astype(jnp.bfloat16)
    grad_heads = heads_first(grad_att, head_count)

    def delta_step(tile_no, rows_in, carried):
        (delta_sum,), shared = carried
        query_rows, pos_in, lse_rows, grad_rows = rows_in
        offset = tile_no * key_tile
        scores, hot = tile_scores(query_rows, pos_in[0], offset)
        prob_tile = jnp.exp(scores - lse_rows[:, :, None])
        value_block = lax.dynamic_slice_in_dim(values_nat, offset, key_tile, 0)
        grad_probs = jnp.einsum(
            "hqd,khd->hqk", grad_rows, value_block, preferred_element_type=jnp.float32
        )
        return ((delta_sum + jnp.sum(prob_tile * grad_probs, axis=2),), shared)

    delta_out = sweep(delta_step, (query_heads, pos_rows, self_lse, grad_heads), (zero_stats,), ())
    self_delta = delta_out[0][0]

    def grad_step(tile_no, rows_in, carried):
        (dquery,), shared = carried
        query_rows, pos_in, lse_rows, grad_rows, delta_rows = rows_in
        offset = tile_no * key_tile
        scores, hot = tile_scores(query_rows, pos_in[0], offset)
        key_block = lax.dynamic_slice_in_dim(keys_nat, offset, key_tile, 0)
        value_block = lax.dynamic_slice_in_dim(values_nat, offset, key_tile, 0)
        prob_tile = jnp.exp(scores - lse_rows[:, :, None])
        grad_probs = jnp.einsum(
            "hqd,khd->hqk", grad_rows, value_block, preferred_element_type=jnp.float32
        )
        dscore = (prob_tile * (grad_probs - delta_rows[:, :, None])).astype(jnp.bfloat16)
        dquery = dquery + jnp.einsum(
            "hqk,khd->hqd", dscore, key_block, preferred_element_type=jnp.float32
        )
        table_acc = shared[0] + jnp.einsum(
            "hqk,qkb->bh", dscore, hot, preferred_element_type=jnp.float32
        )
        return ((dquery,), (table_acc,))

    rows_back = (query_heads, pos_rows, self_lse, grad_heads, self_delta)
    zero_table = jnp.zeros((bucket_count, head_count), jnp.float32)
    grad_out_rows, grad_shared = sweep(grad_step, rows_back, (zero_heads,), (zero_table,))
    table_grad = grad_shared[0]
    query_gath, grad_gath = (
        lax.all_gather(queries, ("ctx", "wsh"), axis=0, tiled=True),
        lax.all_gather(grad_att, ("ctx", "wsh"), axis=0, tiled=True),
    )
    lse_gath, delta_gath = (
        lax.all_gather(self_lse, ("ctx", "wsh"), axis=1, tiled=True),
        lax.all_gather(self_delta, ("ctx", "wsh"), axis=1, tiled=True),
    )
    query_nat = jnp.take(query_gath, device_row, axis=0).reshape(seq_len, head_count, head_size)
    grad_nat = jnp.take(grad_gath, device_row, axis=0).reshape(seq_len, head_count, head_size)
    lse_nat = jnp.take(lse_gath, device_row, axis=1)
    delta_nat = jnp.take(delta_gath, device_row, axis=1)
    own_keys = heads_first(keys_local, head_count)
    own_values = heads_first(values_local, head_count)

    def owner_step(tile_no, key_rows, value_rows, pos_in, key_sums):
        offset = tile_no * key_tile
        query_block = lax.dynamic_slice_in_dim(query_nat, offset, key_tile, 0)
        grad_block = lax.dynamic_slice_in_dim(grad_nat, offset, key_tile, 0)
        lse_block = lax.dynamic_slice_in_dim(lse_nat, offset, key_tile, 1)
        delta_block = lax.dynamic_slice_in_dim(delta_nat, offset, key_tile, 1)
        raw_scores = jnp.einsum(
            "qhd,hkd->hqk", query_block, key_rows, preferred_element_type=jnp.float32
        )
        distance = (offset + jnp.arange(key_tile, dtype=jnp.int32))[:, None] - pos_in[None, :]
        hot = bucket_hot(jnp.maximum(distance, 0))
        scores = jnp.where((distance >= 0)[None], raw_scores + bucket_bias(hot), NEG)
        prob_tile = jnp.exp(scores - lse_block[:, :, None])
        grad_probs = jnp.einsum(
            "qhd,hkd->hqk", grad_block, value_rows, preferred_element_type=jnp.float32
        )
        dscore = (prob_tile * (grad_probs - delta_block[:, :, None])).astype(jnp.bfloat16)
        return (
            key_sums[0]
            + jnp.einsum("hqk,qhd->hkd", dscore, query_block, preferred_element_type=jnp.float32),
            key_sums[1]
            + jnp.einsum(
                "hqk,qhd->hkd",
                prob_tile.astype(jnp.bfloat16),
                grad_block,
                preferred_element_type=jnp.float32,
            ),
        )

    late_start = late_block * block_rows // key_tile
    early_start = early_block * block_rows // key_tile
    both_sums = lax.fori_loop(
        late_start,
        tile_total,
        lambda tile_no, acc_in: owner_step(tile_no, own_keys, own_values, local_pos, acc_in),
        (zero_heads, zero_heads),
    )
    early_sums = lax.fori_loop(
        early_start,
        late_start,
        lambda tile_no, acc_in: owner_step(
            tile_no,
            own_keys[:, :half_rows],
            own_values[:, :half_rows],
            local_pos[:half_rows],
            acc_in,
        ),
        (both_sums[0][:, :half_rows], both_sums[1][:, :half_rows]),
    )
    key_sum = heads_joined(jnp.concatenate([early_sums[0], both_sums[0][:, half_rows:]], axis=1))
    value_sum = heads_joined(jnp.concatenate([early_sums[1], both_sums[1][:, half_rows:]], axis=1))
    dquery_b = heads_joined(grad_out_rows[0]).astype(jnp.bfloat16)
    key_grad_b = key_sum.astype(jnp.bfloat16)
    value_grad_b = value_sum.astype(jnp.bfloat16)
    query_grad = product_tn(normed_one, dquery_b)
    key_grad = product_tn(normed_one, key_grad_b)
    value_grad = product_tn(normed_one, value_grad_b)
    grad_normed_one = (
        product_nt(dquery_b, full_query)
        + product_nt(key_grad_b, full_key)
        + product_nt(value_grad_b, full_value)
    )
    norm_out, norm_pull = jax.vjp(root_norm, x_float, gain_one)
    tokens_part, gain_one_grad = norm_pull(grad_normed_one)
    tokens_grad = grad_one + tokens_part
    (
        query_share,
        key_share,
        value_share,
        out_share,
        cross_query_share,
        cross_key_share,
        cross_value_share,
        cross_out_share,
        gate_share,
        up_share,
        down_share,
    ) = (
        lax.psum_scatter(query_grad, ("ctx", "wsh"), scatter_dimension=1, tiled=True),
        lax.psum_scatter(key_grad, ("ctx", "wsh"), scatter_dimension=1, tiled=True),
        lax.psum_scatter(value_grad, ("ctx", "wsh"), scatter_dimension=1, tiled=True),
        lax.psum_scatter(out_grad, ("ctx", "wsh"), scatter_dimension=0, tiled=True),
        lax.psum_scatter(cross_query_grad, ("ctx", "wsh"), scatter_dimension=1, tiled=True),
        lax.psum_scatter(cross_key_grad, ("ctx", "wsh"), scatter_dimension=1, tiled=True),
        lax.psum_scatter(cross_value_grad, ("ctx", "wsh"), scatter_dimension=1, tiled=True),
        lax.psum_scatter(cross_out_grad, ("ctx", "wsh"), scatter_dimension=0, tiled=True),
        lax.psum_scatter(gate_grad, ("ctx", "wsh"), scatter_dimension=1, tiled=True),
        lax.psum_scatter(up_grad, ("ctx", "wsh"), scatter_dimension=1, tiled=True),
        lax.psum_scatter(down_grad, ("ctx", "wsh"), scatter_dimension=0, tiled=True),
    )
    gain_one_sum, gain_two_sum, gain_three_sum, table_sum = lax.psum(
        (gain_one_grad, gain_two_grad, gain_three_grad, table_grad), ("ctx", "wsh")
    )
    return (
        output,
        tokens_grad,
        encoded_grad,
        gain_one_sum,
        gain_two_sum,
        gain_three_sum,
        query_share,
        key_share,
        value_share,
        out_share,
        cross_query_share,
        cross_key_share,
        cross_value_share,
        cross_out_share,
        gate_share,
        up_share,
        down_share,
        table_sum,
    )


def solution(mesh):
    return jax.shard_map(
        local,
        mesh=mesh,
        in_specs=(
            P(("seq", "ctx", "wsh"), None),
            P(("seq", "ctx", "wsh"), None),
            P(("seq", "ctx", "wsh"), None),
            P(),
            P(),
            P("wsh"),
            P("wsh"),
            P("wsh"),
            P("wsh", None),
            P("wsh", None),
            P("wsh", None),
            P("wsh", None),
            P("wsh", None),
            P("wsh", None),
            P("wsh", None),
            P("wsh", None),
            P("wsh", None),
            P("wsh", None),
            P("wsh", None),
            P(),
        ),
        out_specs=(
            P(("seq", "ctx", "wsh"), None),
            P(("seq", "ctx", "wsh"), None),
            P(("seq", "ctx", "wsh"), None),
            P("seq"),
            P("seq"),
            P("seq"),
            P("seq", ("ctx", "wsh")),
            P("seq", ("ctx", "wsh")),
            P("seq", ("ctx", "wsh")),
            P(("seq", "ctx", "wsh"), None),
            P("seq", ("ctx", "wsh")),
            P("seq", ("ctx", "wsh")),
            P("seq", ("ctx", "wsh")),
            P(("seq", "ctx", "wsh"), None),
            P("seq", ("ctx", "wsh")),
            P("seq", ("ctx", "wsh")),
            P(("seq", "ctx", "wsh"), None),
            P("seq", None),
        ),
        check_vma=False,
    )
```

profile of v0, /device:TPU:0, one launch (start us, length us, event | category | flops | bytes accessed | tf_op | source)
XLA Modules:
  0.0 1838.8 jit_solution(2815211509603276692)
XLA Ops:
  81.8 46.5 %all-gather.38.cloned.1.call-done = bf16[2048,384]{1,0:T(8,128)(2,1)} async-done(((bf16[64,384]{1,0:T(8,128)(2,1)}), bf16[2048,384]{1,0:T(8,128)(2,1)}) %all-gather.38.cloned.1.call-update) | async-done | bytes 1572880 | tf_op jit(solution)/shard_map/all_gather | solution.py:227
  130.9 54.7 %all-gather.34.cloned.1.call-done = bf16[2048,384]{1,0:T(8,128)(2,1)} async-done(((bf16[64,384]{1,0:T(8,128)(2,1)}), bf16[2048,384]{1,0:T(8,128)(2,1)}) %all-gather.34.cloned.1.call-update) | async-done | bytes 1572880 | tf_op jit(solution)/shard_map/all_gather | solution.py:226
  188.2 58.7 %all-gather.26.cloned.1.call-done = bf16[4096,384]{1,0:T(8,128)(2,1)} async-done(((bf16[128,384]{1,0:T(8,128)(2,1)}), bf16[4096,384]{1,0:T(8,128)(2,1)}) %all-gather.26.cloned.1.call-update) | async-done | bytes 3145744 | tf_op jit(solution)/shard_map/all_gather | solution.py:150
  246.8 18.3 gather_fusion.1
  265.1 42.9 %all-gather.20.cloned.1.call-done = bf16[4096,384]{1,0:T(8,128)(2,1)} async-done(((bf16[128,384]{1,0:T(8,128)(2,1)}), bf16[4096,384]{1,0:T(8,128)(2,1)}) %all-gather.20.cloned.1.call-update) | async-done | bytes 3145744 | tf_op jit(solution)/shard_map/all_gather | solution.py:149
  308.1 20.2 %gather_fusion = bf16[4096,384]{1,0:T(8,128)(2,1)} fusion(bf16[4096,384]{1,0:T(8,128)(2,1)} %all-gather.20.cloned.1.call-done, s32[4096]{0:T(1024)} %broadcast_clamp_fusion), kind=kCustom, calls=%fused_computation.clone | custom fusion | bytes 6307840 | tf_op jit(solution)/shard_map/jit(_take)/gather | solution.py:152
  337.3 29.8 %while.114 = (s32[]{:T(128)}, f32[6,128]{1,0:T(8,128)}, f32[6,128]{1,0:T(8,128)}, s32[]{:T(128)}, s32[128]{0:T(128)S(1)}, /*index=5*/bf16[4096,6,64]{0,2,1:T(8,1...) while((s32[]{:T(128)}, f32[6,128]{1,0:T(8,128)}, ...), condition=%wide.region_6.8_spmd, body=%wide.region_3.7_spmd.sunk | while | flops 336072192 | bytes 44241812 | solution.py:171
  369.9 14.2 while.115
  397.0 31.1 %while.116 = (s32[]{:T(128)}, f32[6,128,64]{1,2,0:T(8,128)}, s32[]{:T(128)}, s32[128]{0:T(128)S(1)}, bf16[4096,6,64]{0,2,1:T(8,128)(2,1)S(1)}, /*index=5*/bf16[6...) while((s32[]{:T(128)}, f32[6,128,64]{1,2,0:T(8,128)}, ...), condition=%wide.region_12.14_spmd, body=%wide.region_11.13_spmd.sunk | while | flops 535873536 | bytes 33553220 | solution.py:171
  433.9 14.5 while.117
  537.9 83.4 %reduce-scatter.30.cloned.1.call-done = f32[64,384]{1,0:T(8,128)} async-done(((f32[2048,384]{1,0:T(8,128)}), f32[64,384]{1,0:T(8,128)}) %reduce-scatter.30.cloned.1.call-update) | async-done | bytes 98320
  623.0 104.1 %reduce-scatter.32.cloned.1.call-done = f32[64,384]{1,0:T(8,128)} async-done(((f32[2048,384]{1,0:T(8,128)}), f32[64,384]{1,0:T(8,128)}) %reduce-scatter.32.cloned.1.call-update) | async-done | bytes 98320
  733.2 11.7 fusion.322
  747.8 52.3 %all_gather.85 = f32[6,4096]{0,1:T(8,128)} all-gather(f32[6,128]{0,1:T(8,128)} %add.486), channel_id=1, replica_groups=mesh['seq'=1,'ctx'=16,'wsh'=2] {'ctx','wsh'}, dimensions={1}, use_global_device_ids=true | all-gather | bytes 101376 | tf_op jit(solution)/shard_map/all_gather | solution.py:355
  800.1 17.0 gather_fusion.3
  817.1 19.0 %gather_fusion.2 = bf16[4096,384]{1,0:T(8,128)(2,1)} fusion(bf16[4096,384]{1,0:T(8,128)(2,1)} %all-gather.48.cloned.1.call-done, s32[4096]{0:T(1024)S(1)} %copy-done.74), kind=kCustom, calls=%fused_computation.3.clone | custom fusion | bytes 6307840 | tf_op jit(solution)/shard_map/jit(_take)/gather | solution.py:358
  838.0 29.9 %while.118 = (s32[]{:T(128)}, f32[6,128]{1,0:T(8,128)}, s32[]{:T(128)}, s32[128]{0:T(128)S(1)}, bf16[4096,6,64]{0,2,1:T(8,128)(2,1)S(1)}, /*index=5*/bf16[6,128,...) while((s32[]{:T(128)}, f32[6,128]{1,0:T(8,128)}, ...), condition=%wide.region_24.26_spmd, body=%wide.region_22.25_spmd.sunk | while | flops 537397248 | bytes 71054272 | solution.py:171
  878.2 12.0 fusion.323
  891.5 31.6 %while.120 = (s32[]{:T(128)}, f32[6,128,64]{1,2,0:T(8,128)}, f32[32,6]{0,1:T(8,128)}, s32[]{:T(128)}, s32[128]{0:T(128)S(1)}, /*index=5*/bf16[4096,6,64]{0,2,1:T...) while((s32[]{:T(128)}, f32[6,128,64]{1,2,0:T(8,128)}, ...), condition=%wide.region_29.31_spmd, body=%wide.region_28.30_spmd.sunk | while | flops 866175168 | bytes 74578304 | solution.py:171
  911.9 11.2 fusion.555
  929.0 13.4 while.121
  944.2 47.2 %all_gather.87 = f32[6,4096]{0,1:T(8,128)S(1)} all-gather(f32[6,128]{0,1:T(8,128)S(1)} %copy.283), channel_id=1, replica_groups=mesh['seq'=1,'ctx'=16,'wsh'=2] {'ctx','wsh'}, dimensions={1}, use_global_device_ids=true | all-gather | bytes 101376 | tf_op jit(solution)/shard_map/all_gather | solution.py:356
  991.4 14.1 gather_fusion.5
  1034.2 19.4 %gather_fusion.4 = bf16[4096,384]{1,0:T(8,128)(2,1)} fusion(bf16[4096,384]{1,0:T(8,128)(2,1)} %all-gather.50.cloned.1.call-done, s32[4096]{0:T(1024)S(1)} %copy-done.75), kind=kCustom, calls=%fused_computation.4.clone | custom fusion | bytes 6307840 | tf_op jit(solution)/shard_map/jit(_take)/gather | solution.py:359
  1066.8 29.3 %while.122 = (s32[]{:T(128)}, f32[6,128,64]{1,2,0:T(8,128)S(1)}, f32[6,128,64]{1,2,0:T(8,128)S(1)}, s32[128]{0:T(128)S(1)}, bf16[4096,6,64]{0,2,1:T(8,128)(2,1)}...) while((s32[]{:T(128)}, f32[6,128,64]{1,2,0:T(8,128)S(1)}, ...), condition=%wide.region_33.36_spmd, body=%wide.region_32.35_spmd.sunk | while | flops 943294464 | bytes 44559260 | solution.py:396
  1098.6 16.1 while.123
  1122.9 237.4 %fusion.310 = (f32[1472,16]{0,1:T(8,128)S(1)}, f32[1472,16]{0,1:T(8,128)S(1)}, f32[1472,16]{0,1:T(8,128)S(1)}, f32[16,1472]{1,0:T(8,128)S(1)}, f32[1472,16]{0,1:T(8,128)S(1)}, /*index=5*/f32[16,1472]{1,0:T(8,128)S(1)}) fusion(f32[1472,384]{0,1:T(8,128)} %fusion.305, f32[1472,384]{0,1:T(8,128)} %fusion.303, f32[1472,384]{0,1:T(8,128)} %fusion.301, ...), kind=kCustom, calls=%all-reduce-scatter.6 | all-reduce-scatter fusion | flops 4521985 | bytes 14131200
  1538.0 39.2 %all-reduce.17 = (f32[1472]{0:T(1024)}, f32[1472]{0:T(1024)}, f32[1472]{0:T(1024)}, f32[32,6]{0,1:T(8,128)}) all-reduce(f32[1472]{0:T(1024)S(1)} %get-tuple-element.1256, f32[1472]{0:T(1024)S(1)} %copy-done.146, f32[1472]{0:T(1024)S(1)} %copy-done.145, ...), channel_id=1, replica_groups=mesh['seq'=1,'ctx'=16,'wsh'=2] {'ctx','wsh'}, use_global_device_ids=true, to_apply=%region_40.43 | all-reduce | flops 4608 | bytes 36864 | tf_op jit(solution)/shard_map/psum | solution.py:455
  1591.9 14.4 concatenate.44
  1606.3 13.5 concatenate.45
  1619.9 13.4 concatenate.46
  1645.5 186.5 %reduce-scatter.28.cloned.1.call-done = f32[112,1472]{1,0:T(8,128)} async-done(((f32[3584,1472]{1,0:T(8,128)}), f32[112,1472]{1,0:T(8,128)}) %reduce-scatter.28.cloned.1.call-update) | async-done | bytes 659472 | tf_op jit(solution)/shard_map/reduce_scatter | solution.py:453
  (781 shorter events, 687.5 us)
Async XLA Ops:
  8.7 36.6 %all-gather.24.cloned.1.call-start = ((), (), s32[]{:S(2)}) async-start(), calls=%async_computation.8 | async-start | bytes 1695744 | tf_op jit(solution)/shard_map/all_gather | solution.py:97
  9.5 47.6 %all-gather.18.cloned.1.call-start = ((), (), s32[]{:S(2)}) async-start(), calls=%async_computation.5 | async-start | bytes 1695744 | tf_op jit(solution)/shard_map/all_gather | solution.py:96
  10.1 69.3 %all-gather.22.cloned.1.call-start = ((), (), s32[]{:S(2)}) async-start(), calls=%async_computation.7 | async-start | bytes 1695744 | tf_op jit(solution)/shard_map/all_gather | solution.py:95
  10.6 117.6 %all-gather.38.cloned.1.call-start = ((), (), s32[]{:S(2)}) async-start(), calls=%async_computation.15 | async-start | bytes 1622016 | tf_op jit(solution)/shard_map/all_gather | solution.py:227
  23.7 161.8 %all-gather.34.cloned.1.call-start = ((), (), s32[]{:S(2)}) async-start(), calls=%async_computation.13 | async-start | bytes 1622016 | tf_op jit(solution)/shard_map/all_gather | solution.py:226
  35.6 211.2 %all-gather.26.cloned.1.call-start = ((), (), s32[]{:S(2)}) async-start(), calls=%async_computation.9 | async-start | bytes 3244032 | tf_op jit(solution)/shard_map/all_gather | solution.py:150
  48.0 260.1 %all-gather.20.cloned.1.call-start = ((), (), s32[]{:S(2)}) async-start(), calls=%async_computation.6 | async-start | bytes 3244032 | tf_op jit(solution)/shard_map/all_gather | solution.py:149
  59.7 392.1 %all-gather.28.cloned.1.call-start = ((), (), s32[]{:S(2)}) async-start(), calls=%async_computation.10 | async-start | bytes 1769472 | tf_op jit(solution)/shard_map/all_gather | solution.py:98
  60.3 394.9 %all-gather.30.cloned.1.call-start = ((), (), s32[]{:S(2)}) async-start(), calls=%async_computation.11 | async-start | bytes 1695744 | tf_op jit(solution)/shard_map/all_gather | solution.py:99
  61.1 405.3 %all-gather.40.cloned.1.call-start = ((), (), s32[]{:S(2)}) async-start(), calls=%async_computation.16 | async-start | bytes 1769472 | tf_op jit(solution)/shard_map/all_gather | solution.py:102
  61.6 408.8 %all-gather.42.cloned.1.call-start = ((), (), s32[]{:S(2)}) async-start(), calls=%async_computation.17 | async-start | bytes 15826944 | tf_op jit(solution)/shard_map/all_gather | solution.py:103
  62.4 415.1 %all-gather.44.cloned.1.call-start = ((), (), s32[]{:S(2)}) async-start(), calls=%async_computation.18 | async-start | bytes 15826944 | tf_op jit(solution)/shard_map/all_gather | solution.py:104
  63.0 421.5 %all-gather.46.cloned.1.call-start = ((), (), s32[]{:S(2)}) async-start(), calls=%async_computation.19 | async-start | bytes 15826944 | tf_op jit(solution)/shard_map/all_gather | solution.py:105
  63.6 557.7 %reduce-scatter.30.cloned.1.call-start = ((), (), s32[]{:S(2)}) async-start(), calls=%async_computation.25 | async-start | bytes 3244032
  520.4 206.7 %reduce-scatter.32.cloned.1.call-start = ((), (), s32[]{:S(2)}) async-start(), calls=%async_computation.26 | async-start | bytes 3244032
  529.8 287.3 %all-gather.48.cloned.1.call-start = ((), (), s32[]{:S(2)}) async-start(), calls=%async_computation.20 | async-start | bytes 3244032 | tf_op jit(solution)/shard_map/all_gather | solution.py:351
  530.3 503.9 %all-gather.50.cloned.1.call-start = ((), (), s32[]{:S(2)}) async-start(), calls=%async_computation.21 | async-start | bytes 3244032 | tf_op jit(solution)/shard_map/all_gather | solution.py:352
  537.9 1102.2 %all-reduce.23.cloned.1.call-start = ((), (), s32[]{:S(2)}) async-start(), calls=%async_computation.27 | async-start | bytes 9043968
  732.8 912.7 %reduce-scatter.24.cloned.1.call-start = ((), (), s32[]{:S(2)}) async-start(), calls=%async_computation.22 | async-start | bytes 22708224 | tf_op jit(solution)/shard_map/reduce_scatter | solution.py:451
  745.0 900.5 %reduce-scatter.26.cloned.1.call-start = ((), (), s32[]{:S(2)}) async-start(), calls=%async_computation.23 | async-start | bytes 22708224 | tf_op jit(solution)/shard_map/reduce_scatter | solution.py:452
  890.2 941.8 %reduce-scatter.28.cloned.1.call-start = ((), (), s32[]{:S(2)}) async-start(), calls=%async_computation.24 | async-start | bytes 22708224 | tf_op jit(solution)/shard_map/reduce_scatter | solution.py:453
  1368.7 39.3 %collective-permute-start.6 = (f32[1472,16]{0,1:T(8,128)S(1)}, f32[1472,16]{0,1:T(8,128)}, u32[]{:S(2)}, u32[]{:S(2)}) collective-permute-start(f32[1472,16]{0,1:T(8,128)S(1)} %get-tuple-element.1517), channel_id=1, source_target_pairs={{0,7},{1,8},{2,9},{3,10},{4,11},{5,12},{6,13},{7,14},{8,15},{9,16}... | collective-permute-start | bytes 282632
  1372.5 43.3 %collective-permute-start.5 = (f32[1472,16]{0,1:T(8,128)S(1)}, f32[1472,16]{0,1:T(8,128)}, u32[]{:S(2)}, u32[]{:S(2)}) collective-permute-start(f32[1472,16]{0,1:T(8,128)S(1)} %get-tuple-element.1517), channel_id=1, source_target_pairs={{0,6},{1,7},{2,8},{3,9},{4,10},{5,11},{6,12},{7,13},{8,14},{9,15},... | collective-permute-start | bytes 282632
  1388.1 41.0 %collective-permute-start.4 = (f32[1472,16]{0,1:T(8,128)S(1)}, f32[1472,16]{0,1:T(8,128)S(1)}, u32[]{:S(2)}, u32[]{:S(2)}) collective-permute-start(f32[1472,16]{0,1:T(8,128)S(1)} %get-tuple-element.1517), channel_id=1, source_target_pairs={{0,5},{1,6},{2,7},{3,8},{4,9},{5,10},{6,11},{7,12},{8,13},{9,14},{... | collective-permute-start | bytes 282632
  1395.0 42.3 %collective-permute-start.3 = (f32[1472,16]{0,1:T(8,128)S(1)}, f32[1472,16]{0,1:T(8,128)S(1)}, u32[]{:S(2)}, u32[]{:S(2)}) collective-permute-start(f32[1472,16]{0,1:T(8,128)S(1)} %get-tuple-element.1517), channel_id=1, source_target_pairs={{0,4},{1,5},{2,6},{3,7},{4,8},{5,9},{6,10},{7,11},{8,12},{9,13},{1... | collective-permute-start | bytes 282632
  1402.3 39.6 %collective-permute-start.2 = (f32[1472,16]{0,1:T(8,128)S(1)}, f32[1472,16]{0,1:T(8,128)S(1)}, u32[]{:S(2)}, u32[]{:S(2)}) collective-permute-start(f32[1472,16]{0,1:T(8,128)S(1)} %get-tuple-element.1517), channel_id=1, source_target_pairs={{0,3},{1,4},{2,5},{3,6},{4,7},{5,8},{6,9},{7,10},{8,11},{9,12},{10... | collective-permute-start | bytes 282632
  1408.1 35.1 %collective-permute-start.1 = (f32[1472,16]{0,1:T(8,128)S(1)}, f32[1472,16]{0,1:T(8,128)S(1)}, u32[]{:S(2)}, u32[]{:S(2)}) collective-permute-start(f32[1472,16]{0,1:T(8,128)S(1)} %get-tuple-element.1517), channel_id=1, source_target_pairs={{0,2},{1,3},{2,4},{3,5},{4,6},{5,7},{6,8},{7,9},{8,10},{9,11},{10,... | collective-permute-start | bytes 282632
  1524.0 95.9 %collective-permute-start.44 = (f32[16,1472]{1,0:T(8,128)S(1)}, f32[16,1472]{1,0:T(8,128)}, u32[]{:S(2)}, u32[]{:S(2)}) collective-permute-start(f32[16,1472]{1,0:T(8,128)S(1)} %get-tuple-element.1522), channel_id=1, source_target_pairs={{0,5},{1,6},{2,7},{3,8},{4,9},{5,10},{6,11},{7,12},{8,13},{9,14},{... | collective-permute-start | bytes 282632
  1526.9 93.0 %collective-permute-start.43 = (f32[16,1472]{1,0:T(8,128)S(1)}, f32[16,1472]{1,0:T(8,128)}, u32[]{:S(2)}, u32[]{:S(2)}) collective-permute-start(f32[16,1472]{1,0:T(8,128)S(1)} %get-tuple-element.1522), channel_id=1, source_target_pairs={{0,4},{1,5},{2,6},{3,7},{4,8},{5,9},{6,10},{7,11},{8,12},{9,13},{1... | collective-permute-start | bytes 282632
  1529.0 90.9 %collective-permute-start.42 = (f32[16,1472]{1,0:T(8,128)S(1)}, f32[16,1472]{1,0:T(8,128)}, u32[]{:S(2)}, u32[]{:S(2)}) collective-permute-start(f32[16,1472]{1,0:T(8,128)S(1)} %get-tuple-element.1522), channel_id=1, source_target_pairs={{0,3},{1,4},{2,5},{3,6},{4,7},{5,8},{6,9},{7,10},{8,11},{9,12},{10... | collective-permute-start | bytes 282632
  1532.0 87.9 %collective-permute-start.41 = (f32[16,1472]{1,0:T(8,128)S(1)}, f32[16,1472]{1,0:T(8,128)}, u32[]{:S(2)}, u32[]{:S(2)}) collective-permute-start(f32[16,1472]{1,0:T(8,128)S(1)} %get-tuple-element.1522), channel_id=1, source_target_pairs={{0,2},{1,3},{2,4},{3,5},{4,6},{5,7},{6,8},{7,9},{8,10},{9,11},{10,... | collective-permute-start | bytes 282632
  1534.8 85.1 %collective-permute-start.40 = (f32[16,1472]{1,0:T(8,128)S(1)}, f32[16,1472]{1,0:T(8,128)}, u32[]{:S(2)}, u32[]{:S(2)}) collective-permute-start(f32[16,1472]{1,0:T(8,128)S(1)} %get-tuple-element.1522), channel_id=1, source_target_pairs={{0,1},{1,2},{2,3},{3,4},{4,5},{5,6},{6,7},{7,8},{8,9},{9,10},{10,1... | collective-permute-start | bytes 282632
  (224 other events, 5521.1 us)
Sparse Core Ops, SparseCore 0:
  9.6 11.8 all-gather.35
  23.1 10.3 all-gather.31
  35.0 10.3 all-gather.23
  46.7 10.3 all-gather.17
  58.5 10.3 all-gather.21
  72.1 56.0 all-gather.37
  131.7 53.8 all-gather.33
  189.0 57.8 all-gather.25
  250.3 57.7 all-gather.19
  309.5 8.0 all-gather.27
  319.1 10.3 all-gather.29
  330.8 10.3 all-gather.39
  342.8 24.0 all-gather.41
  368.4 24.0 all-gather.43
  393.9 24.0 all-gather.45
  520.5 100.7 reduce-scatter.29
  626.6 100.4 reduce-scatter.31
  730.4 63.5 all-gather.47
  797.4 58.0 all-gather.49
  861.3 144.8 all-reduce.22
  1014.3 284.3 reduce-scatter.23
  1306.9 293.2 reduce-scatter.25
  1608.3 223.5 reduce-scatter.27
where the time goes:
time: 1850 us; the launch traced here: 1840 us
  waiting for transfers between devices  619 us (33%)
  blocking collectives  379 us (20%)
  local copies, waits for them, and re-layouts  303 us (16%)
  matrix products  302 us (16%)
  starting transfers between devices  161 us (9%)
  other arithmetic  51.8 us (3%)
    unnamed x2, blocking collectives  241 us
    unnamed x74, waiting for transfers between devices  197 us
    reduce_scatter x1, waiting for transfers between devices, local(): lax.psum_scatter(down_grad, ('ctx', 'wsh'), scatter_dimension=0, tiled=True)  186 us
    unnamed x51, starting transfers between devices  160 us
    unnamed x325, local copies, waits for them, and re-layouts  90.8 us
    dot_general x10, matrix products, bucket_bias(): jnp.einsum('qkb,bh->hqk', hot, bucket_table, preferred_element_type=jnp.f...  74.3 us
    all_gather x1, waiting for transfers between devices, local(): lax.all_gather(values_local, ('ctx', 'wsh'), axis=0, tiled=True)  58.7 us
    all_gather x1, waiting for transfers between devices, local(): lax.all_gather(enc_keys_local, ('ctx', 'wsh'), axis=0, tiled=True)  54.7 us
  transfers between devices with their start and end apart: 71, of which 12 were waited for; matrix products, arithmetic and copies ran while one was open for 46% of the time, Pallas kernels for 0%

commit v1 on v0

v1 whole, which is shorter than its diff:
```python
import functools

import jax
import jax.numpy as jnp
from jax import lax
from jax.experimental import pallas as pl
from jax.experimental.pallas import tpu as pltpu
from jax.sharding import PartitionSpec as P

EPS = 1e-06
NEG = -1e30
F32 = jnp.float32
BF = jnp.bfloat16
BLK = 128
GRP = 4
CH = BLK * GRP
VLIM = 60 * 1024 * 1024


def dot(a, b):
    return lax.dot_general(a, b, (((1,), (0,)), ((), ())), preferred_element_type=F32)


def dot_nt(a, b):
    return lax.dot_general(a, b, (((1,), (1,)), ((), ())), preferred_element_type=F32)


def dot_tn(a, b):
    return lax.dot_general(a, b, (((0,), (0,)), ((), ())), preferred_element_type=F32)


def lane_of(shape):
    return lax.broadcasted_iota(jnp.int32, shape, 1)


def head_mask(value, head, hs):
    lane = lane_of(value.shape)
    keep = (lane >= head * hs) & (lane < (head + 1) * hs)
    return jnp.where(keep, value, jnp.zeros_like(value))


def lane_fold(value, op):
    out = value[:, :BLK]
    for i in range(1, value.shape[1] // BLK):
        out = op(out, value[:, i * BLK : (i + 1) * BLK])
    return out


def pieces_into(base, columns, first):
    lane = lane_of(base.shape)
    out = base
    for i, column in enumerate(columns):
        rest = column
        for j in range(3):
            part = rest.astype(BF).astype(F32)
            rest = rest - part
            out = jnp.where(lane == first + 3 * i + j, part, out)
    return out


def params(flops, nbytes, trans):
    return dict(
        compiler_params=pltpu.CompilerParams(vmem_limit_bytes=VLIM),
        cost_estimate=pl.CostEstimate(
            flops=int(flops), bytes_accessed=int(nbytes), transcendentals=int(trans)
        ),
    )


VM = pl.BlockSpec(memory_space=pltpu.VMEM)
SM = pl.BlockSpec(memory_space=pltpu.SMEM)


def bias_kernel(nb, nh, nat_ref, rev_ref, ts_ref, tt_ref):
    r = pl.program_id(0)
    row = lax.broadcasted_iota(jnp.int32, (BLK, BLK), 0)
    col = lax.broadcasted_iota(jnp.int32, (BLK, BLK), 1)

    def skew(first, second):
        line = jnp.concatenate([first, second], axis=1)
        spread = jnp.broadcast_to(line, (BLK, 2 * BLK))
        return pltpu.roll(spread, 0, 1, stride=1, stride_axis=0)[:, :BLK]

    d = nb - 1 - r
    dc = jnp.maximum(d, 0)
    a_all, b_all = rev_ref[nb - dc], rev_ref[nb - dc - 1]
    for h in range(nh):
        tile = skew(a_all[h : h + 1], b_all[h : h + 1])
        tile = jnp.where(d * BLK + row - col >= 0, tile, NEG)
        ts_ref[0, h] = tile.astype(BF)
    d = r - (GRP - 1)
    dc = jnp.maximum(d, 0)
    a_all, b_all = nat_ref[dc + 1], nat_ref[dc]
    for h in range(nh):
        tile = skew(a_all[h : h + 1], b_all[h : h + 1])
        tile = jnp.where(d * BLK + col - row >= 0, tile, NEG)
        tt_ref[0, h] = tile.astype(BF)


def bias_tiles(values):
    nh, length = values.shape
    nb = length // BLK
    zero = jnp.zeros((nh, 1), F32)
    nat = jnp.concatenate([jnp.zeros((nh, BLK), F32), values], axis=1)
    rev = jnp.concatenate([zero, jnp.flip(values, 1), jnp.zeros((nh, BLK - 1), F32)], axis=1)
    nat = jnp.transpose(nat.reshape(nh, nb + 1, BLK), (1, 0, 2))
    rev = jnp.transpose(rev.reshape(nh, nb + 1, BLK), (1, 0, 2))
    rows = nb + GRP - 1
    shape = jax.ShapeDtypeStruct((rows, nh, BLK, BLK), BF)
    spec = pl.BlockSpec((1, nh, BLK, BLK), lambda r: (r, 0, 0, 0))
    return pl.pallas_call(
        functools.partial(bias_kernel, nb, nh),
        grid=(rows,),
        in_specs=[VM, VM],
        out_specs=[spec, spec],
        out_shape=[shape, shape],
        **params(0, 4 * rows * nh * BLK * BLK, 0),
    )(nat, rev)


def gather_blocks(ref, meta_ref, nctx, first, lo, hi):
    parts = []
    for i in range(GRP):
        t = first + i
        early = t < nctx
        slot = meta_ref[jnp.where(early, t, 2 * nctx - 1 - t)]
        parts.append(ref[2 * slot + jnp.where(early, 0, 1), :, lo:hi])
    return jnp.concatenate(parts, axis=0)


def bias_of(ref, first, h):
    return jnp.concatenate([ref[first + i, h] for i in range(GRP)], axis=1).astype(F32)


def self_fwd_kernel(
    nctx, nh, hs, meta_ref, q_ref, kv_ref, ts_ref, o_ref, qe_ref, lse_ref, s_ref, acc_ref
):
    nb = 2 * nctx
    wide = nh * hs
    early = meta_ref[nctx]
    for half in range(2):
        blk = early if half == 0 else nb - 1 - early
        chunks = blk // GRP + 1
        q = q_ref[half * BLK : (half + 1) * BLK, :]
        qm = [head_mask(q, h, hs) for h in range(nh)]

        def score(ch, tops):
            keys = gather_blocks(kv_ref, meta_ref, nctx, ch * GRP, 0, 2 * BLK)
            out = []
            for h in range(nh):
                s = dot_nt(qm[h], keys) + bias_of(ts_ref, nb - 1 - blk + ch * GRP, h)
                s_ref[ch, h] = s
                out.append(jnp.maximum(tops[h], lane_fold(s, jnp.maximum)))
            return tuple(out)

        tops = lax.fori_loop(
            0, chunks, score, tuple(jnp.full((BLK, BLK), NEG, F32) for _ in range(nh))
        )
        tops = [jnp.max(t, axis=1, keepdims=True) for t in tops]
        acc_ref[...] = jnp.zeros_like(acc_ref)

        def weigh(ch, sums):
            vals = gather_blocks(kv_ref, meta_ref, nctx, ch * GRP, BLK, 3 * BLK)
            out = []
            for h in range(nh):
                p = jnp.exp(s_ref[ch, h] - tops[h])
                out.append(sums[h] + lane_fold(p, jnp.add))
                acc_ref[h] += dot(p.astype(BF), vals)
            return tuple(out)

        sums = lax.fori_loop(
            0, chunks, weigh, tuple(jnp.zeros((BLK, BLK), F32) for _ in range(nh))
        )
        sums = [jnp.sum(t, axis=1, keepdims=True) for t in sums]
        total = jnp.zeros((BLK, 2 * BLK), F32)
        for h in range(nh):
            total = total + head_mask(acc_ref[h] / sums[h], h + 1, hs)
        rows = slice(half * BLK, (half + 1) * BLK)
        o_ref[rows, :] = pltpu.roll(total, 2 * BLK - hs, 1)
        lse = [tops[h] + jnp.log(sums[h]) for h in range(nh)]
        lane = lane_of((BLK, BLK))
        cols = jnp.zeros((BLK, BLK), F32)
        for h in range(nh):
            cols = jnp.where(lane == h, lse[h], cols)
        lse_ref[rows, :] = cols
        qe_ref[rows, :] = pieces_into(q.astype(F32), [-t for t in lse], wide).astype(BF)


def self_fwd(meta, q, kv, ts, nh, hs):
    nb = kv.shape[0]
    nctx = nb // 2
    pairs = (nb + 1) * BLK * BLK * nh
    return pl.pallas_call(
        functools.partial(self_fwd_kernel, nctx, nh, hs),
        in_specs=[SM, VM, VM, VM],
        out_specs=[VM, VM, VM],
        out_shape=[
            jax.ShapeDtypeStruct((2 * BLK, 2 * BLK), F32),
            jax.ShapeDtypeStruct((2 * BLK, 2 * BLK), BF),
            jax.ShapeDtypeStruct((2 * BLK, BLK), F32),
        ],
        scratch_shapes=[
            pltpu.VMEM((nb // GRP, nh, BLK, CH), F32),
            pltpu.VMEM((nh, BLK, 2 * BLK), F32),
        ],
        **params(pairs * 2 * 512, 10e6, pairs),
    )(meta, q, kv, ts)


def self_dq_kernel(
    nctx, nh, hs, meta_ref, q_ref, da_ref, lse_ref, del_ref, kv_ref, ts_ref, dq_ref, rev_ref, acc_ref
):
    nb = 2 * nctx
    early = meta_ref[nctx]
    rev_ref[...] = jnp.zeros_like(rev_ref)
    row = lax.broadcasted_iota(jnp.int32, (BLK, BLK), 0)
    col = lax.broadcasted_iota(jnp.int32, (BLK, BLK), 1)
    flip = (row + col == BLK - 1).astype(BF)
    for half in range(2):
        blk = early if half == 0 else nb - 1 - early
        chunks = blk // GRP + 1
        rows = slice(half * BLK, (half + 1) * BLK)
        q = q_ref[rows, :]
        da = da_ref[rows, :]
        qm = [head_mask(q, h, hs) for h in range(nh)]
        dm = [head_mask(da, h + 1, hs) for h in range(nh)]
        lse = [lse_ref[rows, h : h + 1] for h in range(nh)]
        delta = [del_ref[rows, h : h + 1] for h in range(nh)]
        acc_ref[...] = jnp.zeros_like(acc_ref)

        def step(ch, carry):
            both = gather_blocks(kv_ref, meta_ref, nctx, ch * GRP, 0, 3 * BLK)
            keys, vals = both[:, : 2 * BLK], both[:, BLK:]
            off = pl.multiple_of((ch * GRP - blk + nb - 1) * BLK, BLK)
            for h in range(nh):
                s = dot_nt(qm[h], keys) + bias_of(ts_ref, nb - 1 - blk + ch * GRP, h)
                p = jnp.exp(s - lse[h])
                ds = (p * (dot_nt(dm[h], vals) - delta[h])).astype(BF)
                acc_ref[h] += dot(ds, keys)
                flat = jnp.concatenate([dot(flip, ds), jnp.zeros((BLK, BLK), F32)], axis=1)
                flat = pltpu.roll(flat, 0, 1, stride=1, stride_axis=0)
                line = jnp.sum(flat.reshape(BLK // 8, 8, CH + BLK), axis=0)
                rev_ref[h * 8 : (h + 1) * 8, pl.ds(off, CH + BLK)] += line
            return carry

        lax.fori_loop(0, chunks, step, 0)
        total = jnp.zeros((BLK, 2 * BLK), F32)
        for h in range(nh):
            total = total + head_mask(acc_ref[h], h, hs)
        dq_ref[rows, :] = total.astype(BF)


def self_dq(meta, q, da, lse, delta, kv, ts, nh, hs):
    nb = kv.shape[0]
    pairs = (nb + 1) * BLK * BLK * nh
    return pl.pallas_call(
        functools.partial(self_dq_kernel, nb // 2, nh, hs),
        in_specs=[SM] + [VM] * 6,
        out_specs=[VM, VM],
        out_shape=[
            jax.ShapeDtypeStruct((2 * BLK, 2 * BLK), BF),
            jax.ShapeDtypeStruct((8 * nh, nb * BLK + CH), F32),
        ],
        scratch_shapes=[pltpu.VMEM((nh, BLK, 2 * BLK), F32)],
        **params(pairs * 2 * 896, 10e6, pairs),
    )(meta, q, da, lse, delta, kv, ts)


def self_dkv_kernel(
    nctx, nh, hs, meta_ref, k_ref, v_ref, qg_ref, dg_ref, tt_ref, dk_ref, dv_ref, ka_ref, va_ref
):
    nb = 2 * nctx
    wide = nh * hs
    early = meta_ref[nctx]

    def extended(value, h):
        lane = lane_of(value.shape)
        first = wide + 3 * h
        ones = (lane >= first) & (lane < first + 3)
        return jnp.where(ones, jnp.ones_like(value), head_mask(value, h, hs))

    for half in range(2):
        blk = early if half == 0 else nb - 1 - early
        rows = slice(half * BLK, (half + 1) * BLK)
        km = [extended(k_ref[rows, :], h) for h in range(nh)]
        vm = [extended(v_ref[rows, :], h) for h in range(nh)]
        ka_ref[...] = jnp.zeros_like(ka_ref)
        va_ref[...] = jnp.zeros_like(va_ref)

        def step(ch, carry):
            qc = gather_blocks(qg_ref, meta_ref, nctx, ch * GRP, 0, 2 * BLK)
            dc = gather_blocks(dg_ref, meta_ref, nctx, ch * GRP, 0, 2 * BLK)
            for h in range(nh):
                s = dot_nt(km[h], qc) + bias_of(tt_ref, ch * GRP - blk + GRP - 1, h)
                p = jnp.exp(s)
                ds = (p * dot_nt(vm[h], dc)).astype(BF)
                ka_ref[h] += dot(ds, qc)
                va_ref[h] += dot(p.astype(BF), dc)
            return carry

        lax.fori_loop(blk // GRP, nb // GRP, step, 0)
        dk = jnp.zeros((BLK, 2 * BLK), F32)
        dv = jnp.zeros((BLK, 2 * BLK), F32)
        for h in range(nh):
            dk = dk + head_mask(ka_ref[h], h, hs)
            dv = dv + head_mask(va_ref[h], h, hs)
        dk_ref[rows, :] = dk.astype(BF)
        dv_ref[rows, :] = dv.astype(BF)


def self_dkv(meta, k, v, qg, dg, tt, nh, hs):
    nb = qg.shape[0]
    pairs = (nb + 1) * BLK * BLK * nh
    shape = jax.ShapeDtypeStruct((2 * BLK, 2 * BLK), BF)
    return pl.pallas_call(
        functools.partial(self_dkv_kernel, nb // 2, nh, hs),
        in_specs=[SM] + [VM] * 5,
        out_specs=[VM, VM],
        out_shape=[shape, shape],
        scratch_shapes=[pltpu.VMEM((nh, BLK, 2 * BLK), F32)] * 2,
        **params(pairs * 2 * 1024, 10e6, pairs),
    )(meta, k, v, qg, dg, tt)


def cross_fwd_kernel(nh, hs, q_ref, e_ref, o_ref, qe_ref, s_ref):
    wide = nh * hs
    chunks = e_ref.shape[0] // CH
    for half in range(2):
        rows = slice(half * BLK, (half + 1) * BLK)
        q = q_ref[rows, :]
        total = jnp.zeros((BLK, 2 * BLK), F32)
        lse = []
        for h in range(nh):
            qm = head_mask(q, h, hs)
            top = jnp.full((BLK, BLK), NEG, F32)
            for ch in range(chunks):
                s = dot_nt(qm, e_ref[ch * CH : (ch + 1) * CH, : 2 * BLK])
                s_ref[ch] = s
                top = jnp.maximum(top, lane_fold(s, jnp.maximum))
            top = jnp.max(top, axis=1, keepdims=True)
            summed = jnp.zeros((BLK, BLK), F32)
            acc = jnp.zeros((BLK, 2 * BLK), F32)
            for ch in range(chunks):
                p = jnp.exp(s_ref[ch] - top)
                summed = summed + lane_fold(p, jnp.add)
                acc = acc + dot(p.astype(BF), e_ref[ch * CH : (ch + 1) * CH, 2 * BLK :])
            summed = jnp.sum(summed, axis=1, keepdims=True)
            total = total + head_mask(acc / summed, h, hs)
            lse.append(top + jnp.log(summed))
        o_ref[rows, :] = total
        qe_ref[rows, :] = pieces_into(q.astype(F32), [-t for t in lse], wide).astype(BF)


def cross_fwd(q, e, nh, hs):
    pairs = 2 * BLK * e.shape[0] * nh
    return pl.pallas_call(
        functools.partial(cross_fwd_kernel, nh, hs),
        in_specs=[VM, VM],
        out_specs=[VM, VM],
        out_shape=[
            jax.ShapeDtypeStruct((2 * BLK, 2 * BLK), F32),
            jax.ShapeDtypeStruct((2 * BLK, 2 * BLK), BF),
        ],
        scratch_shapes=[pltpu.VMEM((e.shape[0] // CH, BLK, CH), F32)],
        **params(pairs * 2 * 512, 4e6, pairs),
    )(q, e)


def cross_bwd_kernel(nh, hs, qe_ref, de_ref, e_ref, dq_ref, dke_ref, dve_ref, acc_ref):
    wide = nh * hs
    ch = pl.program_id(0)

    @pl.when(ch == 0)
    def _():
        acc_ref[...] = jnp.zeros_like(acc_ref)

    ek = e_ref[:, : 2 * BLK]
    ev = e_ref[:, 2 * BLK :]
    ek_t = jnp.transpose(ek.astype(F32)).astype(BF)

    def kept(value, h):
        lane = lane_of(value.shape)
        first = wide + 3 * h
        keep = ((lane >= h * hs) & (lane < (h + 1) * hs)) | ((lane >= first) & (lane < first + 3))
        return jnp.where(keep, value, jnp.zeros_like(value))

    dk = jnp.zeros((e_ref.shape[0], 2 * BLK), F32)
    dv = jnp.zeros((e_ref.shape[0], 2 * BLK), F32)
    for h in range(nh):
        qm = kept(qe_ref[...], h)
        dm = kept(de_ref[...], h)
        p = jnp.exp(dot_nt(ek, qm))
        ds = (p * dot_nt(ev, dm)).astype(BF)
        dk = dk + dot(ds, qm)
        dv = dv + dot(p.astype(BF), dm)
        acc_ref[h * hs : (h + 1) * hs, :] += dot(ek_t[h * hs : (h + 1) * hs, :], ds)
    dke_ref[...] = dk.astype(BF)
    dve_ref[...] = dv.astype(BF)

    @pl.when(ch == pl.num_programs(0) - 1)
    def _():
        dq_ref[...] = acc_ref[...].astype(BF)


def cross_bwd(qe, de, e, nh, hs):
    rows = e.shape[0]
    pairs = 2 * BLK * rows * nh
    const = pl.BlockSpec((2 * BLK, 2 * BLK), lambda i: (0, 0))
    part = pl.BlockSpec((CH, 2 * BLK), lambda i: (i, 0))
    shape = jax.ShapeDtypeStruct((rows, 2 * BLK), BF)
    return pl.pallas_call(
        functools.partial(cross_bwd_kernel, nh, hs),
        grid=(rows // CH,),
        in_specs=[const, const, pl.BlockSpec((CH, 4 * BLK), lambda i: (i, 0))],
        out_specs=[pl.BlockSpec((nh * hs, 2 * BLK), lambda i: (0, 0)), part, part],
        out_shape=[jax.ShapeDtypeStruct((nh * hs, 2 * BLK), BF), shape, shape],
        scratch_shapes=[pltpu.VMEM((nh * hs, 2 * BLK), F32)],
        **params(pairs * 2 * 1024, 4e6, pairs),
    )(qe, de, e)


def grad_prep_kernel(nh, hs, dy_ref, w_ref, o_ref, de_ref, dh_ref, del_ref):
    wide = nh * hs
    da = dot_nt(dy_ref[...], w_ref[...]).astype(BF)
    terms = da.astype(F32) * o_ref[...]
    delta = [jnp.sum(head_mask(terms, h, hs), axis=1, keepdims=True) for h in range(nh)]
    dh_ref[...] = pltpu.roll(da.astype(F32), hs, 1).astype(BF)
    lane = lane_of(del_ref.shape)
    cols = jnp.zeros(del_ref.shape, F32)
    for h in range(nh):
        cols = jnp.where(lane == h, delta[h], cols)
    del_ref[...] = cols
    de_ref[...] = pieces_into(da.astype(F32), [-t for t in delta], wide).astype(BF)


def grad_prep(dy, weight, o, nh, hs):
    rows = dy.shape[0]
    padded = jnp.pad(weight, ((0, 2 * BLK - weight.shape[0]), (0, 0)))
    shape = jax.ShapeDtypeStruct((rows, 2 * BLK), BF)
    return pl.pallas_call(
        functools.partial(grad_prep_kernel, nh, hs),
        in_specs=[VM] * 3,
        out_specs=[VM] * 3,
        out_shape=[shape, shape, jax.ShapeDtypeStruct((rows, BLK), F32)],
        **params(2 * rows * 2 * BLK * dy.shape[1], 2e6, 0),
    )(dy, padded, o)


def scale_of(rows):
    return lax.rsqrt(jnp.mean(rows * rows, axis=-1, keepdims=True) + EPS)


def norm_back(rows, gain, grad):
    rr = scale_of(rows)
    scaled = gain * grad
    shared = jnp.mean(rows * scaled, axis=-1, keepdims=True)
    dv = rr * scaled - rows * (rr * rr * rr) * shared
    return dv, jnp.sum(rows * rr * grad, axis=0)


def local(
    tokens,
    encoded,
    cotangent,
    assign,
    bucket_ids,
    gain_self,
    gain_cross,
    gain_ffn,
    query_weight,
    key_weight,
    value_weight,
    out_weight,
    cross_query,
    cross_key,
    cross_value,
    cross_out,
    gate_weight,
    up_weight,
    down_weight,
    bucket_table,
):
    nctx = lax.axis_size("ctx")
    nw = lax.axis_size("wsh")
    c = lax.axis_index("ctx")
    w = lax.axis_index("wsh")
    both = ("ctx", "wsh")
    rows, width = tokens.shape
    half = rows // 2
    length = rows * nw * nctx
    buckets, heads = bucket_table.shape
    inner = query_weight.shape[1]
    hs = inner // heads
    nh = heads // nw
    wide = nh * hs
    plane = 4
    nz = nctx // plane
    spot = (c % plane) * nw + w
    zed = c // plane
    hidden = gate_weight.shape[1]
    share = hidden // (nctx * nw)

    def pair(x, axis=0, tiled=True):
        return lax.all_gather(x, "wsh", axis=axis, tiled=tiled)

    def own_heads(x, axis):
        return lax.dynamic_slice_in_dim(x, w * wide, wide, axis)

    def chip_order(x):
        x = x.reshape((nw, 2, half) + x.shape[1:])
        return jnp.swapaxes(x, 0, 1).reshape((2 * nw * half,) + x.shape[3:])

    def own_rows(x):
        x = x.reshape((2, nw, half) + x.shape[1:])
        x = lax.dynamic_index_in_dim(x, w, 1, keepdims=False)
        return x.reshape((2 * half,) + x.shape[2:])

    def near(x, k):
        return lax.ppermute(x, "ctx", [(i, i ^ k) for i in range(nctx)])

    def plane_gather(x):
        parts = jnp.stack([x] + [near(x, k) for k in range(1, plane)])
        return pair(parts, tiled=False).reshape((nw * plane * x.shape[0],) + x.shape[1:])

    def plane_scatter(partial):
        parts = partial.reshape(nw, plane, rows, width)
        mine = lax.dynamic_index_in_dim(parts, w, 0, keepdims=False)
        other = lax.dynamic_index_in_dim(parts, 1 - w, 0, keepdims=False).astype(BF)
        swap = [(i, (i + 1) % nw) for i in range(nw)]
        mine = mine + lax.ppermute(other, "wsh", swap).astype(F32)
        total = mine[0]
        for k in range(1, plane):
            total = total + near(mine[k].astype(BF), k).astype(F32)
        return total

    def zed_scatter(parts):
        total = lax.dynamic_index_in_dim(parts, zed, 0, keepdims=False)
        for k in range(1, nz):
            piece = lax.dynamic_index_in_dim(parts, (zed + k) % nz, 0, keepdims=False)
            perm = [(i, ((i // plane + k) % nz) * plane + i % plane) for i in range(nctx)]
            total = total + lax.ppermute(piece.astype(BF), "ctx", perm).astype(F32)
        return total

    lanes = jnp.arange(nctx, dtype=jnp.int32)
    owner = jnp.sum(jnp.where(assign[None, :] == lanes[:, None], lanes[None, :], 0), axis=1)
    meta = jnp.concatenate([owner, jnp.take(assign, c)[None]]).astype(jnp.int32)

    gains = pair(jnp.stack([gain_self, gain_cross, gain_ffn]), axis=1).astype(F32)
    tok = chip_order(pair(tokens)).astype(F32)
    qkv_full = pair(jnp.concatenate([query_weight, key_weight, value_weight], axis=1))
    qkv_heads = jnp.concatenate(
        [own_heads(qkv_full[:, i * inner : (i + 1) * inner], 1) for i in range(3)], axis=1
    )
    n1 = (tok * scale_of(tok) * gains[0]).astype(BF)
    qkv = dot(n1, qkv_heads).astype(BF)
    lane_pad = ((0, 0), (0, 2 * BLK - wide))
    q = jnp.pad(qkv[:, :wide], lane_pad)
    k_own = jnp.pad(qkv[:, wide : 2 * wide], lane_pad)
    v_own = jnp.pad(qkv[:, 2 * wide :], lane_pad)
    kv = lax.all_gather(qkv[:, wide:], "ctx", axis=0, tiled=True)
    kv = kv.reshape(2 * nctx, BLK, 2 * wide)

    enc_pair = pair(encoded)
    ck_full, cv_full, cq_full = pair(cross_key), pair(cross_value), pair(cross_query)
    ekv_heads = jnp.concatenate([own_heads(ck_full, 1), own_heads(cv_full, 1)], axis=1)
    ekv = dot(enc_pair, ekv_heads).astype(BF)
    ones = jnp.ones((ekv.shape[0], 2 * BLK - wide), BF)
    ekv = jnp.concatenate([ekv[:, :wide], ones, ekv[:, wide:], ones], axis=1)
    ekv = lax.all_gather(ekv, "ctx", axis=0, tiled=True)

    hot = (bucket_ids[None, :] == jnp.arange(buckets, dtype=jnp.int32)[:, None]).astype(BF)
    values = dot_tn(lax.dynamic_slice_in_dim(bucket_table, w * nh, nh, 1), hot)
    ts, tt = bias_tiles(values)

    def units(matrix, index):
        parts = [
            lax.dynamic_slice_in_dim(matrix, (z * plane * nw + index) * share, share, 1)
            for z in range(nz)
        ]
        return jnp.concatenate(parts, axis=1)

    mates = [(c % plane) * nw + i for i in range(nw)]
    up_gate = jnp.stack(
        [jnp.concatenate([units(gate_weight, m), units(up_weight, m)], axis=1) for m in mates]
    )
    up_gate = lax.all_to_all(up_gate, "wsh", 0, 0, tiled=True)
    up_gate = up_gate.reshape(width, 2 * nz * share)
    wg, wu = up_gate[:, : nz * share], up_gate[:, nz * share :]
    down_parts = down_weight.reshape(nz // nw, plane * nw, share, width)
    wd = jnp.stack([lax.dynamic_index_in_dim(down_parts, m, 1, keepdims=False) for m in mates])
    wd = lax.all_to_all(wd, "wsh", 0, 0, tiled=True).reshape(nz * share, width)

    out_full, cross_out_full = pair(out_weight), pair(cross_out)
    g_plane = plane_gather(cotangent)

    o1, qe1, lse1 = self_fwd(meta, q, kv, ts, nh, hs)
    a1_heads = o1[:, :wide].astype(BF)
    a1 = jnp.swapaxes(pair(a1_heads, tiled=False), 0, 1).reshape(nw * rows, inner)
    h1 = tok + dot(a1, out_full)
    n2 = (h1 * scale_of(h1) * gains[1]).astype(BF)
    cq = jnp.pad(dot(n2, own_heads(cq_full, 1)).astype(BF), lane_pad)
    qg = lax.all_gather(qe1, "ctx", axis=0, tiled=True).reshape(2 * nctx, BLK, 2 * BLK)

    o2, qe2 = cross_fwd(cq, ekv, nh, hs)
    a2 = pair(o2[:, :wide].astype(BF), tiled=False)
    a2 = own_rows(jnp.swapaxes(a2, 0, 1).reshape(nw * rows, inner))
    h1_own = own_rows(h1)
    h2 = h1_own + dot(a2, cross_out_full)
    n3 = (h2 * scale_of(h2) * gains[2]).astype(BF)

    n3_plane = plane_gather(n3)
    gate = dot(n3_plane, wg)
    up = dot(n3_plane, wu)
    act = (jax.nn.gelu(gate, approximate=True) * up).astype(BF)
    dact = dot_nt(g_plane, wd)
    _, pull = jax.vjp(lambda a, b: jax.nn.gelu(a, approximate=True) * b, gate, up)
    dgate, dup = pull(dact)
    dgate, dup = dgate.astype(BF), dup.astype(BF)
    dn3 = plane_scatter(dot_nt(dgate, wg) + dot_nt(dup, wu))
    output = (h2 + plane_scatter(dot(act, wd))).astype(BF)
    ffn = jnp.concatenate(
        [
            dot_tn(m, v).astype(BF).reshape(nz, share, width)
            for m, v in ((dgate, n3_plane), (dup, n3_plane), (act, g_plane))
        ],
        axis=1,
    )
    ffn = zed_scatter(ffn)
    dh2_part, gain3 = norm_back(h2, gains[2], dn3)
    dh2 = cotangent.astype(F32) + dh2_part

    dy2 = dh2.astype(BF)
    de2, _, _ = grad_prep(chip_order(pair(dy2)), cross_out, o2, nh, hs)
    dcq_t, dek, dev = cross_bwd(qe2, de2, ekv, nh, hs)
    dcq = jnp.swapaxes(pair(dcq_t, tiled=True), 0, 1)
    dcq_own = own_rows(dcq)
    dn2 = dot_nt(dcq_own, cq_full)
    dh1_part, gain2 = norm_back(h1_own, gains[1], dn2)
    dh1 = dh2 + dh1_part
    dekv = jnp.concatenate([dek[:, :wide], dev[:, :wide]], axis=1)
    dekv = lax.psum_scatter(dekv, "ctx", scatter_dimension=0, tiled=True)
    dekv = pair(dekv, tiled=False)
    dekv = lax.dynamic_slice_in_dim(dekv, w * encoded.shape[0], encoded.shape[0], 1)
    dek_own = jnp.swapaxes(dekv[:, :, :wide], 0, 1).reshape(encoded.shape[0], inner)
    dev_own = jnp.swapaxes(dekv[:, :, wide:], 0, 1).reshape(encoded.shape[0], inner)
    encoded_grad = dot_nt(dek_own, ck_full) + dot_nt(dev_own, cv_full)

    dy1 = dh1.astype(BF)
    de1, dhi1, delta1 = grad_prep(chip_order(pair(dy1)), out_weight, o1, nh, hs)
    dg = lax.all_gather(de1, "ctx", axis=0, tiled=True).reshape(2 * nctx, BLK, 2 * BLK)
    dq, rev = self_dq(meta, q, dhi1, lse1, delta1, kv, ts, nh, hs)
    dk, dv = self_dkv(meta, k_own, v_own, qg, dg, tt, nh, hs)
    dqkv = jnp.concatenate([dq[:, :wide], dk[:, :wide], dv[:, :wide]], axis=1)
    dqkv = jnp.swapaxes(pair(dqkv, tiled=False), 0, 1)
    dqkv = own_rows(dqkv).reshape(rows, nw, 3, wide)
    dqkv = jnp.swapaxes(dqkv, 1, 2).reshape(rows, 3 * inner)
    dn1 = dot_nt(dqkv, qkv_full)
    tok_part, gain1 = norm_back(tokens.astype(F32), gains[0], dn1)
    tokens_grad = dh1 + tok_part

    by_distance = jnp.sum(rev.reshape(nh, 8, -1), axis=1)[:, :length]
    hot_rev = (
        jnp.flip(bucket_ids)[None, :] == jnp.arange(buckets, dtype=jnp.int32)[:, None]
    ).astype(F32)
    table_own = lax.dot_general(
        hot_rev, by_distance, (((1,), (1,)), ((), ())), precision=lax.Precision.HIGHEST
    )
    table = lax.dynamic_update_slice_in_dim(
        jnp.zeros((buckets, heads), F32), table_own, w * nh, 1
    )

    def to_owners(grads):
        each = [g.astype(BF).reshape(nctx * nw, inner // (nctx * nw), width) for g in grads]
        joined = jnp.concatenate(each, axis=1)
        extra = -joined.shape[1] % 16
        joined = jnp.pad(joined, ((0, 0), (0, extra), (0, 0)))
        got = lax.psum_scatter(joined, both, scatter_dimension=0, tiled=True)[0].astype(F32)
        each = inner // (nctx * nw)
        return [got[i * each : (i + 1) * each] for i in range(len(grads))]

    n1_own, n2_own, a1_own = own_rows(n1), own_rows(n2), own_rows(a1)
    out_share, cross_out_share, cq_t, ck_t, cv_t = to_owners(
        [
            dot_tn(a1_own, dy1),
            dot_tn(a2, dy2),
            dot_tn(dcq_own, n2_own),
            dot_tn(dek_own, encoded),
            dot_tn(dev_own, encoded),
        ]
    )
    q_t, k_t, v_t = to_owners(
        [dot_tn(dqkv[:, i * inner : (i + 1) * inner], n1_own) for i in range(3)]
    )
    gain1, gain2, gain3, table = lax.psum((gain1, gain2, gain3, table), both)
    return (
        output,
        tokens_grad,
        encoded_grad,
        gain1,
        gain2,
        gain3,
        q_t.T,
        k_t.T,
        v_t.T,
        out_share,
        cq_t.T,
        ck_t.T,
        cv_t.T,
        cross_out_share,
        ffn[:share].T,
        ffn[share : 2 * share].T,
        ffn[2 * share :],
        table,
    )


def solution(mesh):
    rows = P(("seq", "ctx", "wsh"), None)
    cols = P("seq", ("ctx", "wsh"))
    split = P("wsh", None)
    return jax.shard_map(
        local,
        mesh=mesh,
        in_specs=(rows, rows, rows, P(), P(), P("wsh"), P("wsh"), P("wsh"))
        + (split,) * 11
        + (P(),),
        out_specs=(
            rows,
            rows,
            rows,
            P("seq"),
            P("seq"),
            P("seq"),
            cols,
            cols,
            cols,
            rows,
            cols,
            cols,
            cols,
            rows,
            cols,
            cols,
            rows,
            P("seq", None),
        ),
        check_vma=False,
    )
```

time: 1850 us -> 928 us (0.50)
  blocking collectives: 379 us -> 86.3 us
  matrix products: 302 us -> 66 us
  waiting for transfers between devices: 619 us -> 396 us
  starting transfers between devices: 161 us -> 29.5 us
  local copies, waits for them, and re-layouts: 303 us -> 202 us
  Pallas kernels: 0 us -> 76.1 us
    unnamed x2 -> x0, blocking collectives: 241 us -> none
    dot_general x71 -> x28, matrix products: 302 us -> 66 us  [the longest x7 26.6 us: dot_nt(): lax.dot_general(a, b, (((1,), (1,)), ((), ())), preferred_element_type=F32)]
    unnamed x74 -> x15, waiting for transfers between devices: 197 us -> 3.3 us
    unnamed x51 -> x0, starting transfers between devices: 160 us -> none
    ppermute x0 -> x17, waiting for transfers between devices: none -> 112 us  [the longest x3 68.5 us: zed_scatter(): total = total + lax.ppermute(piece.astype(BF), 'ctx', perm).astype(F32)]
    gather x7 -> x0, local copies, waits for them, and re-layouts: 109 us -> none  [the longest x1 20.2 us: local(): jnp.take(keys_all, device_row, axis=0)]
    all_gather x2 -> x10, blocking collectives: 99.5 us -> 23.4 us  [pair(): return lax.all_gather(x, 'wsh', axis=axis, tiled=tiled)]
    pallas_call x0 -> x8, Pallas kernels: none -> 76.1 us  [the longest x1 15.6 us: bias_tiles(): pl.pallas_call(functools.partial(bias_kernel, nb, nh), grid=(rows,), in_s...]
  transfers between devices with their start and end apart: 71 -> 34, of which waited for: 12 -> 17; matrix products, arithmetic and copies ran while one was open for 46% -> 29% of each run, Pallas kernels for 0% -> 8%
where the time goes in v1:
time: 928 us; the launch traced here: 917 us
  waiting for transfers between devices  396 us (43%)
  local copies, waits for them, and re-layouts  202 us (22%)
  blocking collectives  86.3 us (9%)
  Pallas kernels  76.1 us (8%)
  matrix products  66 us (7%)
  other arithmetic  45.3 us (5%)
  starting transfers between devices  29.5 us (3%)
  between operations  16.2 us (2%)
    reduce_scatter x1, waiting for transfers between devices, local(): dekv = lax.psum_scatter(dekv, 'ctx', scatter_dimension=0, tiled=True)  72.1 us
    ppermute x3, waiting for transfers between devices, zed_scatter(): total = total + lax.ppermute(piece.astype(BF), 'ctx', perm).astype(F32)  68.5 us
    psum x1, blocking collectives, local(): gain1, gain2, gain3, table = lax.psum((gain1, gain2, gain3, table), both)  62.9 us
    all_gather x1, waiting for transfers between devices, local(): ekv = lax.all_gather(ekv, 'ctx', axis=0, tiled=True)  62.1 us
    concatenate x1, local copies, waits for them, and re-layouts, to_owners(): joined = jnp.concatenate(each, axis=1)  56.8 us
    reduce_scatter x2, waiting for transfers between devices, to_owners(): lax.psum_scatter(joined, both, scatter_dimension=0, tiled=True)[0]  43.5 us
    ppermute x12, waiting for transfers between devices, near(): return lax.ppermute(x, 'ctx', [(i, i ^ k) for i in range(nctx)])  43.3 us
    all_gather x1, waiting for transfers between devices, local(): kv = lax.all_gather(qkv[:, wide:], 'ctx', axis=0, tiled=True)  43 us
  transfers between devices with their start and end apart: 34, of which 17 were waited for; matrix products, arithmetic and copies ran while one was open for 29% of the time, Pallas kernels for 8%

profile of v1, /device:TPU:0, one launch (start us, length us, event | category | flops | bytes accessed | tf_op | source)
XLA Modules:
  0.0 917.1 jit_solution(10811895807854404404)
XLA Ops:
  18.2 7.2 all-gather.20.cloned.1.call-done
  38.8 10.3 %all-gather.28.cloned.1.call-done = bf16[1472,384]{1,0:T(8,128)(2,1)} async-done(((bf16[736,384]{1,0:T(8,128)(2,1)}), bf16[1472,384]{1,0:T(8,128)(2,1)}) %all-gather.28.cloned.1.call-update) | async-done | bytes 1130512 | tf_op jit(solution)/shard_map/all_gather | solution.py:504
  62.5 15.6 %shard_map.331 = (bf16[35,3,128,128]{3,2,1,0:T(8,128)(2,1)}, bf16[35,3,128,128]{3,2,1,0:T(8,128)(2,1)}) custom-call(f32[33,3,128]{2,1,0:T(4,128)} %pad_bitcast_fusion.nat_ref, f32[33,3,128]{2,1,0:T(4,128)} %bitcast.331), custom_call_target="tpu_custom_call" | custom-call | bytes 6881280 | tf_op jit(solution)/shard_map/pallas_call | solution.py:111
  78.7 43.0 %all-gather.22.cloned.1.call-done = bf16[4096,384]{1,0:T(8,128)(2,1)} async-done(((bf16[256,384]{1,0:T(8,128)(2,1)}), bf16[4096,384]{1,0:T(8,128)(2,1)}) %all-gather.22.cloned.1.call-update) | async-done | bytes 3145744 | tf_op jit(solution)/shard_map/all_gather | solution.py:560
  121.8 10.9 %shard_map.332 = (f32[256,256]{1,0:T(8,128)}, bf16[256,256]{1,0:T(8,128)(2,1)}, f32[256,128]{1,0:T(8,128)}) custom-call(s32[17]{0:T(128)} %pad_add_fusion.meta_ref, bf16[256,256]{1,0:T(8,128)(2,1)} %slice_select_fusion.q_ref, bf16[32,128,384]{2,1,0:T(8,128)(2,1)} %bitcast.294, bf16[35,3,128,128]{3,2,1,0:T(8,128)(2,1)} %get-tuple-element.36.ts_ref), custom_call_target="tpu_custom_call" | custom-call | flops 1660944384 | bytes 10000000 | tf_op jit(solution)/shard_map/pallas_call | solution.py:193
  145.8 62.1 %all-gather.32.cloned.1.call-done.e_ref = bf16[2048,512]{1,0:T(8,128)(2,1)} async-done(((bf16[128,512]{1,0:T(8,128)(2,1)}), bf16[2048,512]{1,0:T(8,128)(2,1)}) %all-gather.32.cloned.1.call-update) | async-done | bytes 2097168 | tf_op jit(solution)/shard_map/all_gather | solution.py:569
  207.9 6.7 shard_map.333
  227.6 7.9 collective-permute-done
  235.5 8.5 collective-permute-done.1
  248.9 8.2 collective-permute-done.7
  257.1 6.5 collective-permute-done.8
  265.0 5.7 constant_dynamic-slice_fusion.16
  281.9 5.0 all-to-all-start
  286.9 8.2 copy.224
  302.9 5.8 fusion.13
  313.0 7.1 multiply_convert_fusion
  323.9 5.9 convolution_add_fusion
  329.8 6.5 copy.227
  376.3 4.7 collective-permute-done.11
  382.2 7.6 collective-permute-done.13
  402.6 7.4 shard_map.335
  436.1 15.3 %shard_map.337 = (bf16[256,256]{1,0:T(8,128)(2,1)}, f32[24,4608]{1,0:T(8,128)}) custom-call(s32[17]{0:T(128)} %pad_add_fusion.meta_ref, bf16[256,256]{1,0:T(8,128)(2,1)} %slice_select_fusion.q_ref, bf16[256,256]{1,0:T(8,128)(2,1)} %get-tuple-element.42.da_ref, f32[256,128]{1,0:T(8,128)} %get-tuple-element.43.lse_ref, f32[256,128]{1,0:T(8,128)} %get-tuple-element.44.del_ref, ...), custom_call_target="tpu_custom_call" | custom-call | flops 2906652672 | bytes 10000000 | tf_op jit(solution)/shard_map/pallas_call | solution.py:256
  451.5 38.8 %all-gather.38.cloned.1.call-done = bf16[4096,256]{1,0:T(8,128)(2,1)} async-done(((bf16[256,256]{1,0:T(8,128)(2,1)}), bf16[4096,256]{1,0:T(8,128)(2,1)}) %all-gather.38.cloned.1.call-update) | async-done | bytes 2097168 | tf_op jit(solution)/shard_map/all_gather | solution.py:650
  490.2 14.3 %shard_map.338 = (bf16[256,256]{1,0:T(8,128)(2,1)}, bf16[256,256]{1,0:T(8,128)(2,1)}) custom-call(s32[17]{0:T(128)} %pad_add_fusion.meta_ref, bf16[256,256]{1,0:T(8,128)(2,1)} %pad.33.k_ref, bf16[256,256]{1,0:T(8,128)(2,1)} %pad.34.v_ref, bf16[32,128,256]{2,1,0:T(8,128)(2,1)} %bitcast.338, bf16[32,128,256]{2,1,0:T(8,128)(2,1)} %bitcast.339, ...), custom_call_target="tpu_custom_call" | custom-call | flops 3321888768 | bytes 10000000 | tf_op jit(solution)/shard_map/pallas_call | solution.py:315
  523.5 4.9 fusion.4
  546.3 72.1 %reduce-scatter.4.cloned.1.call-done = bf16[128,384]{1,0:T(8,128)(2,1)} async-done(((bf16[2048,384]{1,0:T(8,128)(2,1)}), bf16[128,384]{1,0:T(8,128)(2,1)}) %reduce-scatter.4.cloned.1.call-update) | async-done | bytes 98320 | tf_op jit(solution)/shard_map/reduce_scatter | solution.py:641
  636.7 56.8 %concatenate.54 = bf16[32,60,1472]{2,1,0:T(8,128)(2,1)} concatenate(bf16[32,12,1472]{2,1,0:T(8,128)(2,1)S(1)} %reshape.339, bf16[32,12,1472]{2,1,0:T(8,128)(2,1)} %reshape.340, bf16[32,12,1472]{2,1,0:T(8,128)(2,1)S(1)} %reshape.344, bf16[32,12,1472]{2,1,0:T(8,128)(2,1)} %reshape.345, bf16[32,12,1472]{2,1,0:T(8,128)(2,1)} %reshape.346), dimensions={1} | concatenate | bytes 11304960 | tf_op jit(solution)/shard_map/concatenate | solution.py:674
  693.5 6.4 pad.36
  717.9 24.9 %collective-permute-done.14 = bf16[336,1472]{1,0:T(8,128)(2,1)S(1)} collective-permute-done((bf16[336,1472]{1,0:T(8,128)(2,1)}, bf16[336,1472]{1,0:T(8,128)(2,1)S(1)}, u32[]{:S(2)}, u32[]{:S(2)}) %collective-permute-start.14) | collective-permute-done | bytes 989216 | tf_op jit(solution)/shard_map/ppermute | solution.py:541
  742.8 43.5 %collective-permute-done.15 = bf16[336,1472]{1,0:T(8,128)(2,1)S(1)} collective-permute-done((bf16[336,1472]{1,0:T(8,128)(2,1)}, bf16[336,1472]{1,0:T(8,128)(2,1)S(1)}, u32[]{:S(2)}, u32[]{:S(2)}) %collective-permute-start.15) | collective-permute-done | bytes 989216 | tf_op jit(solution)/shard_map/ppermute | solution.py:541
  797.6 62.9 %all-reduce.8 = (f32[1472]{0:T(1024)}, f32[1472]{0:T(1024)}, f32[1472]{0:T(1024)}, f32[32,6]{0,1:T(8,128)}) all-reduce(f32[1472]{0:T(1024)S(1)} %get-tuple-element.69, f32[1472]{0:T(1024)S(1)} %copy-done.33, f32[1472]{0:T(1024)S(1)} %copy-done.32, ...), channel_id=1, replica_groups=mesh['seq'=1,'ctx'=16,'wsh'=2] {'ctx','wsh'}, use_global_device_ids=true, to_apply=%region_11.12 | all-reduce | flops 4608 | bytes 36864 | tf_op jit(solution)/shard_map/psum | solution.py:694
  864.8 43.5 %reduce-scatter.8.cloned.1.call-done = bf16[1,64,1472]{2,1,0:T(8,128)(2,1)} async-done(((bf16[32,64,1472]{2,1,0:T(8,128)(2,1)}), bf16[1,64,1472]{2,1,0:T(8,128)(2,1)}) %reduce-scatter.8.cloned.1.call-update) | async-done | bytes 188432 | tf_op jit(solution)/shard_map/reduce_scatter | solution.py:677
  (337 shorter events, 266.6 us)
Async XLA Ops:
  7.2 18.2 %all-gather.20.cloned.1.call-start = ((), (), s32[]{:S(2)}) async-start(), calls=%async_computation.5 | async-start | bytes 5087232 | tf_op jit(solution)/shard_map/all_gather | solution.py:504
  10.0 27.2 %all-gather.30.cloned.1.call-start = ((), (), s32[]{:S(2)}) async-start(), calls=%async_computation.10 | async-start | bytes 1695744 | tf_op jit(solution)/shard_map/all_gather | solution.py:504
  10.8 38.4 %all-gather.28.cloned.1.call-start = ((), (), s32[]{:S(2)}) async-start(), calls=%async_computation.9 | async-start | bytes 1695744 | tf_op jit(solution)/shard_map/all_gather | solution.py:504
  11.5 110.2 %all-gather.22.cloned.1.call-start = ((), (), s32[]{:S(2)}) async-start(), calls=%async_computation.6 | async-start | bytes 3342336 | tf_op jit(solution)/shard_map/all_gather | solution.py:560
  31.3 104.7 %all-gather.24.cloned.1.call-start = ((), (), s32[]{:S(2)}) async-start(), calls=%async_computation.7 | async-start | bytes 1769472 | tf_op jit(solution)/shard_map/all_gather | solution.py:504
  31.9 110.8 %all-gather.26.cloned.1.call-start = ((), (), s32[]{:S(2)}) async-start(), calls=%async_computation.8 | async-start | bytes 1695744 | tf_op jit(solution)/shard_map/all_gather | solution.py:504
  32.5 175.5 %all-gather.32.cloned.1.call-start = ((), (), s32[]{:S(2)}) async-start(), calls=%async_computation.11 | async-start | bytes 2228224 | tf_op jit(solution)/shard_map/all_gather | solution.py:569
  52.2 169.4 %all-gather.34.cloned.1.call-start = ((), (), s32[]{:S(2)}) async-start(), calls=%async_computation.12 | async-start | bytes 1769472 | tf_op jit(solution)/shard_map/all_gather | solution.py:504
  53.0 249.9 %all-gather.40.cloned.1.call-start = ((), (), s32[]{:S(2)}) async-start(), calls=%async_computation.18 | async-start | bytes 4521984 | tf_op jit(solution)/shard_map/all_gather | solution.py:504
  225.3 18.6 %collective-permute-start.1 = (bf16[128,1472]{0,1:T(8,128)(2,1)S(1)}, bf16[128,1472]{0,1:T(8,128)(2,1)S(1)}, u32[]{:S(2)}, u32[]{:S(2)}) collective-permute-start(bf16[128,1472]{0,1:T(8,128)(2,1)S(1)} %multiply_convert_fusion.5), channel_id=1, source_target_pairs={{0,4},{2,6},{4,0},{6,2},{8,12},{10,14},{12,8},{14,10},{16,20},{18,... | collective-permute-start | bytes 1130504 | tf_op jit(solution)/shard_map/ppermute | solution.py:519
  226.0 17.9 %collective-permute-start.2 = (bf16[128,1472]{0,1:T(8,128)(2,1)S(1)}, bf16[128,1472]{0,1:T(8,128)(2,1)S(1)}, u32[]{:S(2)}, u32[]{:S(2)}) collective-permute-start(bf16[128,1472]{0,1:T(8,128)(2,1)S(1)} %multiply_convert_fusion.5), channel_id=1, source_target_pairs={{0,6},{2,4},{4,2},{6,0},{8,14},{10,12},{12,10},{14,8},{16,22},{18,... | collective-permute-start | bytes 1130504 | tf_op jit(solution)/shard_map/ppermute | solution.py:519
  245.3 67.7 %all-gather.42.cloned.1.call-start = ((), (), s32[]{:S(2)}) async-start(), calls=%async_computation.19 | async-start | bytes 4521984 | tf_op jit(solution)/shard_map/all_gather | solution.py:504
  245.3 11.8 %collective-permute-start.7 = (bf16[128,1472]{0,1:T(8,128)(2,1)S(1)}, bf16[128,1472]{0,1:T(8,128)(2,1)S(1)}, u32[]{:S(2)}, u32[]{:S(2)}) collective-permute-start(bf16[128,1472]{0,1:T(8,128)(2,1)S(1)} %copy-done.15), channel_id=1, source_target_pairs={{0,2},{2,0},{4,6},{6,4},{8,10},{10,8},{12,14},{14,12},{16,18},{18,... | collective-permute-start | bytes 1130504 | tf_op jit(solution)/shard_map/ppermute | solution.py:519
  246.0 17.6 %collective-permute-start.8 = (bf16[128,1472]{0,1:T(8,128)(2,1)S(1)}, bf16[128,1472]{0,1:T(8,128)(2,1)S(1)}, u32[]{:S(2)}, u32[]{:S(2)}) collective-permute-start(bf16[128,1472]{0,1:T(8,128)(2,1)S(1)} %copy-done.15), channel_id=1, source_target_pairs={{0,4},{2,6},{4,0},{6,2},{8,12},{10,14},{12,8},{14,10},{16,20},{18,... | collective-permute-start | bytes 1130504 | tf_op jit(solution)/shard_map/ppermute | solution.py:519
  247.5 16.1 %collective-permute-start.9 = (bf16[128,1472]{0,1:T(8,128)(2,1)S(1)}, bf16[128,1472]{0,1:T(8,128)(2,1)S(1)}, u32[]{:S(2)}, u32[]{:S(2)}) collective-permute-start(bf16[128,1472]{0,1:T(8,128)(2,1)S(1)} %copy-done.15), channel_id=1, source_target_pairs={{0,6},{2,4},{4,2},{6,0},{8,14},{10,12},{12,10},{14,8},{16,22},{18,... | collective-permute-start | bytes 1130504 | tf_op jit(solution)/shard_map/ppermute | solution.py:519
  281.9 15.9 %all-to-all-start = ((bf16[2,736,896]{2,1,0:T(8,128)(2,1)}), bf16[2,736,896]{2,1,0:T(8,128)(2,1)}, u32[]{:S(2)}, u32[]{:S(2)}) async-start(bf16[2,736,896]{2,1,0:T(8,128)(2,1)} %pad_maximum_fusion.1), calls=%async_computation | async-start | bytes 5275648 | tf_op jit(solution)/shard_map/all_to_all | solution.py:586
  297.8 15.2 %all-to-all-start.1 = ((bf16[2,2,112,1472]{3,2,1,0:T(8,128)(2,1)}), bf16[2,2,112,1472]{3,2,1,0:T(8,128)(2,1)}, u32[]{:S(2)}, u32[]{:S(2)}) async-start(bf16[2,2,112,1472]{3,2,1,0:T(8,128)(2,1)} %pad_maximum_fusion.6), calls=%async_computation.1 | async-start | bytes 2752512 | tf_op jit(solution)/shard_map/all_to_all | solution.py:591
  302.4 149.1 %all-gather.36.cloned.1.call-start = ((), (), s32[]{:S(2)}) async-start(), calls=%async_computation.13 | async-start | bytes 2228224 | tf_op jit(solution)/shard_map/all_gather | solution.py:602
  342.1 20.8 %collective-permute-start.10 = (bf16[4,128,1472]{1,2,0:T(8,128)(2,1)}, bf16[4,128,1472]{1,2,0:T(8,128)(2,1)}, u32[]{:S(2)}, u32[]{:S(2)}) collective-permute-start(bf16[4,128,1472]{1,2,0:T(8,128)(2,1)} %bitcast.303), channel_id=1, source_target_pairs={{0,1},{1,0},{2,3},{3,2},{4,5},{5,4},{6,7},{7,6},{8,9},{9,8},{10,11... | collective-permute-start | bytes 4521992 | tf_op jit(solution)/shard_map/ppermute | solution.py:530
  346.8 143.5 %all-gather.38.cloned.1.call-start = ((), (), s32[]{:S(2)}) async-start(), calls=%async_computation.14 | async-start | bytes 2228224 | tf_op jit(solution)/shard_map/all_gather | solution.py:650
  365.7 15.3 %collective-permute-start.11 = (bf16[128,1472]{0,1:T(8,128)(2,1)S(1)}, bf16[128,1472]{0,1:T(8,128)(2,1)S(1)}, u32[]{:S(2)}, u32[]{:S(2)}) collective-permute-start(bf16[128,1472]{0,1:T(8,128)(2,1)S(1)} %get-tuple-element.117), channel_id=1, source_target_pairs={{0,2},{2,0},{4,6},{6,4},{8,10},{10,8},{12,14},{14,12},{16,18},{18,... | collective-permute-start | bytes 1130504 | tf_op jit(solution)/shard_map/ppermute | solution.py:519
  367.3 14.9 %collective-permute-start.12 = (bf16[128,1472]{0,1:T(8,128)(2,1)S(1)}, bf16[128,1472]{0,1:T(8,128)(2,1)S(1)}, u32[]{:S(2)}, u32[]{:S(2)}) collective-permute-start(bf16[128,1472]{0,1:T(8,128)(2,1)S(1)} %get-tuple-element.119), channel_id=1, source_target_pairs={{0,4},{2,6},{4,0},{6,2},{8,12},{10,14},{12,8},{14,10},{16,20},{18,... | collective-permute-start | bytes 1130504 | tf_op jit(solution)/shard_map/ppermute | solution.py:519
  367.5 22.3 %collective-permute-start.13 = (bf16[128,1472]{0,1:T(8,128)(2,1)S(1)}, bf16[128,1472]{0,1:T(8,128)(2,1)S(1)}, u32[]{:S(2)}, u32[]{:S(2)}) collective-permute-start(bf16[128,1472]{0,1:T(8,128)(2,1)S(1)} %get-tuple-element.118), channel_id=1, source_target_pairs={{0,6},{2,4},{4,2},{6,0},{8,14},{10,12},{12,10},{14,8},{16,22},{18,... | collective-permute-start | bytes 1130504 | tf_op jit(solution)/shard_map/ppermute | solution.py:519
  374.7 44.0 %collective-permute-start.4 = (bf16[128,1472]{0,1:T(8,128)(2,1)}, bf16[128,1472]{0,1:T(8,128)(2,1)}, u32[]{:S(2)}, u32[]{:S(2)}) collective-permute-start(bf16[128,1472]{0,1:T(8,128)(2,1)} %get-tuple-element.120), channel_id=1, source_target_pairs={{0,2},{2,0},{4,6},{6,4},{8,10},{10,8},{12,14},{14,12},{16,18},{18,... | collective-permute-start | bytes 1130504 | tf_op jit(solution)/shard_map/ppermute | solution.py:519
  376.1 42.5 %collective-permute-start.5 = (bf16[128,1472]{0,1:T(8,128)(2,1)}, bf16[128,1472]{0,1:T(8,128)(2,1)}, u32[]{:S(2)}, u32[]{:S(2)}) collective-permute-start(bf16[128,1472]{0,1:T(8,128)(2,1)} %get-tuple-element.122), channel_id=1, source_target_pairs={{0,4},{2,6},{4,0},{6,2},{8,12},{10,14},{12,8},{14,10},{16,20},{18,... | collective-permute-start | bytes 1130504 | tf_op jit(solution)/shard_map/ppermute | solution.py:519
  381.0 37.7 %collective-permute-start.6 = (bf16[128,1472]{0,1:T(8,128)(2,1)}, bf16[128,1472]{0,1:T(8,128)(2,1)}, u32[]{:S(2)}, u32[]{:S(2)}) collective-permute-start(bf16[128,1472]{0,1:T(8,128)(2,1)} %get-tuple-element.121), channel_id=1, source_target_pairs={{0,6},{2,4},{4,2},{6,0},{8,14},{10,12},{12,10},{14,8},{16,22},{18,... | collective-permute-start | bytes 1130504 | tf_op jit(solution)/shard_map/ppermute | solution.py:519
  430.3 188.1 %reduce-scatter.4.cloned.1.call-start = ((), (), s32[]{:S(2)}) async-start(), calls=%async_computation.15 | async-start | bytes 1671168 | tf_op jit(solution)/shard_map/reduce_scatter | solution.py:641
  433.7 429.4 %reduce-scatter.6.cloned.1.call-start = ((), (), s32[]{:S(2)}) async-start(), calls=%async_computation.16 | async-start | bytes 4866048 | tf_op jit(solution)/shard_map/reduce_scatter | solution.py:677
  528.5 379.8 %reduce-scatter.8.cloned.1.call-start = ((), (), s32[]{:S(2)}) async-start(), calls=%async_computation.17 | async-start | bytes 6488064 | tf_op jit(solution)/shard_map/reduce_scatter | solution.py:677
  711.9 30.9 %collective-permute-start.14 = (bf16[336,1472]{1,0:T(8,128)(2,1)}, bf16[336,1472]{1,0:T(8,128)(2,1)S(1)}, u32[]{:S(2)}, u32[]{:S(2)}) collective-permute-start(bf16[336,1472]{1,0:T(8,128)(2,1)} %get-tuple-element.105), channel_id=1, source_target_pairs={{0,8},{2,10},{4,12},{6,14},{8,16},{10,18},{12,20},{14,22},{16,24},... | collective-permute-start | bytes 2967560 | tf_op jit(solution)/shard_map/ppermute | solution.py:541
  713.1 73.2 %collective-permute-start.15 = (bf16[336,1472]{1,0:T(8,128)(2,1)}, bf16[336,1472]{1,0:T(8,128)(2,1)S(1)}, u32[]{:S(2)}, u32[]{:S(2)}) collective-permute-start(bf16[336,1472]{1,0:T(8,128)(2,1)} %get-tuple-element.107), channel_id=1, source_target_pairs={{0,16},{2,18},{4,20},{6,22},{8,24},{10,26},{12,28},{14,30},{16,0},... | collective-permute-start | bytes 2967560 | tf_op jit(solution)/shard_map/ppermute | solution.py:541
  714.8 71.6 %collective-permute-start.16 = (bf16[336,1472]{1,0:T(8,128)(2,1)}, bf16[336,1472]{1,0:T(8,128)(2,1)S(1)}, u32[]{:S(2)}, u32[]{:S(2)}) collective-permute-start(bf16[336,1472]{1,0:T(8,128)(2,1)} %get-tuple-element.106), channel_id=1, source_target_pairs={{0,24},{2,26},{4,28},{6,30},{8,0},{10,2},{12,4},{14,6},{16,8},{18,... | collective-permute-start | bytes 2967560 | tf_op jit(solution)/shard_map/ppermute | solution.py:541
  (51 other events, 409.8 us)
Sparse Core Ops, SparseCore 0:
  10.1 15.1 all-gather.19
  26.9 10.3 all-gather.29
  38.8 10.3 all-gather.27
  52.4 69.3 all-gather.21
  123.1 7.7 all-gather.23
  132.3 10.3 all-gather.25
  146.0 61.8 all-gather.31
  209.5 7.8 all-gather.33
  245.4 10.5 all-gather.39
  265.1 10.4 all-gather.41
  346.9 69.6 all-gather.35
  430.4 59.7 all-gather.37
  495.0 123.2 reduce-scatter.3
  623.7 144.4 reduce-scatter.5
  774.6 133.5 reduce-scatter.7
